TPU v7x, 128 devices: a whole 4x4x4 slice. The times are simulated.
128 devices in a mesh: row: 32 (over z, y, core), col: 4 (over x).
Axes of the slice: x: 4, y: 4, z: 4, core: 2. Of those that a mesh axis runs over, the one named last changes fastest.
Arguments:
- features: float32 [131072, 128], P('row'), may hold values from -6 to 6
- inv_length: float32 [128], replicated, may hold values from 0.03 to 0.3
- nugget: float32 [131072], P('row'), may hold values from 0.5 to 1.5
- pairs: int32 [2, 131072], replicated, may hold values from 0 to 131071, as said below
- weights: float32 [131072], replicated, may hold values from 0.2 to 2
Outputs:
- factor: float32 [2, 131072, 512], P(None, 'row', 'col')
- schur: float32 [131072, 512], P('row', 'col')
Inputs may be any that keep to these rules, and one draw needn't show every extreme that they name: `pairs`: every configuration is the winner of exactly one pair; a pair's loser minus its winner, modulo 131072, lies in 1 to 1023.
All inputs are finite; a program needn't handle non-finite values.
Results may differ from a plain program's by a relative error of at most 0.0003.
Values sent between devices are 32-bit elements; how exact they have to be, the bound alone decides.
No kernel may reach another device: no remote copies, remote signals or barrier semaphores. Data moves between devices by JAX's collectives and lax.ppermute only.
A program may use at most 192 MiB of HBM per device.

v0:
```python
import math

import jax
import jax.numpy as jnp
from jax import lax
from jax.sharding import PartitionSpec as P

PANEL = 512


signal_variance = 2.0


def spread(value, axis, root):
    mine = lax.axis_index(axis) == root
    return lax.psum(jnp.where(mine, value, jnp.zeros_like(value)), axis)


def kernel_block(scaled, columns):
    own_sq = jnp.sum(scaled * scaled, axis=1)
    col_sq = jnp.sum(columns * columns, axis=1)
    inner = jnp.einsum("if,jf->ij", scaled, columns, precision=lax.Precision.HIGHEST)
    distance = own_sq[:, None] + col_sq[None, :] - 2.0 * inner
    return signal_variance * jnp.exp(-0.5 * distance)


def pair_lookup(glob_ids, winner, losing, weights):
    id_count = glob_ids.shape[0]
    block_len = math.gcd(id_count, 128)
    grouped = glob_ids.reshape(id_count // block_len, block_len)

    def lookup_block(id_block):
        won_mask = id_block[:, None] == winner[None, :]
        won_weight = jnp.sum(jnp.where(won_mask, weights[None, :], jnp.float32(0.0)), axis=1)
        partner_id = jnp.sum(jnp.where(won_mask, losing[None, :], jnp.int32(0)), axis=1)
        lost_mask = id_block[:, None] == losing[None, :]
        lost_weight = jnp.sum(jnp.where(lost_mask, weights[None, :], jnp.float32(0.0)), axis=1)
        return (won_weight, partner_id, lost_weight)

    won_weight, partner_id, lost_weight = lax.map(lookup_block, grouped)
    return (
        won_weight.reshape(id_count),
        partner_id.reshape(id_count),
        lost_weight.reshape(id_count),
    )


def per_device(features, inv_length, nugget, pairs, weights):
    rows_dev = features.shape[0]
    row_rank = lax.axis_index("row")
    col_rank = lax.axis_index("col")
    narrow = PANEL // lax.axis_size("col")
    scaled = features * inv_length[None, :]
    received = []
    col_base = col_rank * narrow
    own_block = lax.dynamic_slice_in_dim(scaled[:PANEL], col_base, narrow, 0)
    for target in range(3):
        received.append(spread(own_block, "row", target))
    columns = jnp.concatenate(received, 0)
    system = kernel_block(scaled, columns)
    row_base = row_rank * rows_dev
    own_ids = row_base + jnp.arange(rows_dev, dtype=jnp.int32)
    col_ids = jnp.concatenate(
        [target * rows_dev + col_base + jnp.arange(narrow, dtype=jnp.int32) for target in range(3)]
    )
    winner, losing = (pairs[0], pairs[1])
    row_won, row_partner, row_lost = pair_lookup(own_ids, winner, losing, weights)
    col_won, col_partner, col_lost = pair_lookup(col_ids, winner, losing, weights)
    same_cell = own_ids[:, None] == col_ids[None, :]
    diagonal_add = jnp.where(
        same_cell, nugget[:, None] + (col_won + col_lost)[None, :], jnp.float32(0.0)
    )
    row_side = jnp.where(
        row_partner[:, None] == col_ids[None, :], row_won[:, None], jnp.float32(0.0)
    )
    col_side = jnp.where(
        col_partner[None, :] == own_ids[:, None], col_won[None, :], jnp.float32(0.0)
    )
    system = system + (diagonal_add - row_side - col_side)
    blocks = [system[:, target * narrow : (target + 1) * narrow] for target in range(3)]
    in_panel = jnp.arange(rows_dev, dtype=jnp.int32) < PANEL
    finished = jnp.zeros((rows_dev,), dtype=bool)
    identity = jnp.eye(PANEL, dtype=jnp.float32)
    outputs = []
    for source in range(2):
        current = blocks[source]
        gathered = lax.all_gather(current, "col", axis=1, tiled=True)
        lowest = jnp.linalg.cholesky(gathered[:PANEL])
        inverse = jax.scipy.linalg.solve_triangular(lowest, identity, lower=True)
        inverse = spread(inverse, "row", source)
        factor = jnp.einsum("rk,jk->rj", gathered, inverse, precision=lax.Precision.HIGHEST)
        is_owner = row_rank == source
        factor = jnp.concatenate([jnp.where(is_owner, lowest, factor[:PANEL]), factor[PANEL:]], 0)
        outputs.append(lax.dynamic_slice_in_dim(factor, col_rank * narrow, narrow, 1))
        finished = finished | is_owner & in_panel
        for target in range(source + 1, 3):
            shared = lax.dynamic_slice_in_dim(factor[:PANEL], col_rank * narrow, narrow, 0)
            shared = spread(shared, "row", target)
            update = jnp.einsum("rk,jk->rj", factor, shared, precision=lax.Precision.HIGHEST)
            blocks[target] = jnp.where(finished[:, None], jnp.float32(0.0), blocks[target] - update)
    schur = blocks[2]
    return (jnp.stack(outputs), schur)


def solution(mesh):
    placed = (P("row", None), P(), P("row"), P(), P())
    return jax.shard_map(
        per_device,
        mesh=mesh,
        in_specs=placed,
        out_specs=(P(None, "row", "col"), P("row", "col")),
        check_vma=False,
    )
```

profile of v0, /device:TPU:1, one launch (start us, length us, event | category | flops | bytes accessed | tf_op | source)
XLA Modules:
  0.0 1760.5 jit_solution(14346753613980356927)
XLA Ops:
  14.2 81.2 %while.30 = (s32[]{:T(128)}, f32[3,128]{1,0:T(4,128)S(1)}, s32[3,128]{1,0:T(4,128)S(1)}, f32[3,128]{1,0:T(4,128)S(1)}, s32[3,128]{1,0:T(4,128)S(1)}, /*index=5*/...) while((s32[]{:T(128)}, f32[3,128]{1,0:T(4,128)S(1)}, ...), condition=%wide.region_9.10_spmd, body=%wide.region_5.9_spmd.sunk | while | flops 150994560 | bytes 2628213 | solution.py:40
  14.2 16.9 select_reduce_fusion.10
  41.3 16.9 select_reduce_fusion.10
  68.3 16.9 select_reduce_fusion.10
  95.4 648.1 %while.31 = (s32[]{:T(128)}, f32[32,128]{1,0:T(8,128)S(1)}, s32[32,128]{1,0:T(8,128)S(1)}, s32[32,128]{1,0:T(8,128)S(1)}, s32[1,131072]{1,0:T(1,128)S(1)}, /*ind...) while((s32[]{:T(128)}, f32[32,128]{1,0:T(8,128)S(1)}, s32[32,128]{1,0:T(8,128)S(1)}, ...), condition=%wide.region_13.14_spmd, body=%wide.region_10.13_spmd.sunk | while | flops 100663040 | bytes 2102377 | solution.py:40
  95.5 10.1 fusion.117
  115.7 10.1 fusion.117
  136.0 10.1 fusion.117
  156.2 10.1 fusion.117
  166.3 10.1 fusion.118
  176.5 10.1 fusion.117
  196.7 10.1 fusion.117
  206.8 10.1 fusion.118
  217.0 10.1 fusion.117
  237.2 10.1 fusion.117
  257.5 10.1 fusion.117
  277.7 10.1 fusion.117
  298.0 10.1 fusion.117
  308.1 10.1 fusion.118
  318.2 10.1 fusion.117
  338.5 10.1 fusion.117
  348.6 10.1 fusion.118
  358.7 10.1 fusion.117
  379.0 10.1 fusion.117
  399.2 10.1 fusion.117
  419.5 10.1 fusion.117
  439.8 10.1 fusion.117
  460.0 10.1 fusion.117
  480.3 10.1 fusion.117
  500.5 10.1 fusion.117
  520.8 10.1 fusion.117
  541.0 10.1 fusion.117
  561.3 10.1 fusion.117
  581.5 10.1 fusion.117
  601.8 10.1 fusion.117
  622.0 10.1 fusion.117
  642.3 10.1 fusion.117
  662.5 10.1 fusion.117
  682.8 10.1 fusion.117
  703.0 10.1 fusion.117
  723.3 10.1 fusion.117
  746.3 10.2 subtract_add_fusion
  761.1 85.9 %all-gather.3.cloned.1.call-done = f32[4096,512]{0,1:T(8,128)} async-done(((f32[4096,128]{0,1:T(8,128)}), f32[4096,512]{0,1:T(8,128)}) %all-gather.3.cloned.1.call-update) | async-done | bytes 8388624 | tf_op jit(solution)/shard_map/all_gather | solution.py:87
  850.1 11.7 cholesky.286
  874.4 11.7 cholesky.305
  899.0 11.7 cholesky.326
  922.6 11.9 cholesky.343
  946.8 40.1 %custom-call.30 = f32[4,128,128]{1,2,0:T(8,128)S(1)} custom-call(f32[4,128,128]{2,1,0:T(8,128)} %copy-done.12), custom_call_target="InvertDiagBlocksLowerTriangular" | custom-call | tf_op jit(solution)/shard_map/jit(_solve_triangular)/triangular_solve | solution.py:89
  991.3 106.0 %all-reduce.9.cloned.1.call-done = f32[512,512]{1,0:T(8,128)} async-done(((f32[512,512]{1,0:T(8,128)}), f32[512,512]{1,0:T(8,128)}) %all-reduce.9.cloned.1.call-update) | async-done | bytes 1048592 | tf_op jit(solution)/shard_map/psum | solution.py:16
  1097.3 28.6 %fusion.90 = f32[4096,512]{1,0:T(8,128)S(1)} fusion(f32[4096,512]{0,1:T(8,128)} %all-gather.3.cloned.1.call-done, f32[512,512]{1,0:T(8,128)} %all-reduce.9.cloned.1.call-done), kind=kOutput, calls=%fused_computation.196 | convolution fusion | flops 12884901888 | bytes 17825792 | tf_op jit(solution)/shard_map/rk,jk->rj/dot_general | solution.py:91
  1137.7 94.0 %all-reduce.11.cloned.1.call-done = f32[128,512]{1,0:T(8,128)} async-done(((f32[128,512]{1,0:T(8,128)}), f32[128,512]{1,0:T(8,128)}) %all-reduce.11.cloned.1.call-update) | async-done | bytes 262160 | tf_op jit(solution)/shard_map/psum | solution.py:16
  1231.7 13.8 fusion.11
  1245.8 82.5 %all-gather.5.cloned.1.call-done = f32[4096,512]{0,1:T(8,128)} async-done(((f32[4096,128]{0,1:T(8,128)}), f32[4096,512]{0,1:T(8,128)}) %all-gather.5.cloned.1.call-update) | async-done | bytes 8388624 | tf_op jit(solution)/shard_map/all_gather | solution.py:87
  1334.5 11.7 cholesky.358
  1358.7 11.7 cholesky.377
  1383.4 11.7 cholesky.398
  1407.0 11.7 cholesky.415
  1423.4 11.5 while.33
  1435.6 40.1 %custom-call.34 = f32[4,128,128]{1,2,0:T(8,128)S(1)} custom-call(f32[4,128,128]{2,1,0:T(8,128)} %copy-done.11), custom_call_target="InvertDiagBlocksLowerTriangular" | custom-call | tf_op jit(solution)/shard_map/jit(_solve_triangular)/triangular_solve | solution.py:89
  1485.7 103.0 %all-reduce.13.cloned.1.call-done = f32[512,512]{1,0:T(8,128)} async-done(((f32[512,512]{1,0:T(8,128)}), f32[512,512]{1,0:T(8,128)}) %all-reduce.13.cloned.1.call-update) | async-done | bytes 1048592 | tf_op jit(solution)/shard_map/psum | solution.py:16
  1588.7 28.7 %fusion.91 = f32[4096,512]{1,0:T(8,128)S(1)} fusion(f32[4096,512]{0,1:T(8,128)} %all-gather.5.cloned.1.call-done, f32[512,512]{1,0:T(8,128)} %all-reduce.13.cloned.1.call-done), kind=kOutput, calls=%fused_computation.197 | convolution fusion | flops 12884901888 | bytes 17825792 | tf_op jit(solution)/shard_map/rk,jk->rj/dot_general | solution.py:91
  1627.9 99.2 %all-reduce.15.cloned.1.call-done = (f32[128,512]{1,0:T(8,128)}, f32[128,512]{1,0:T(8,128)}) async-done(((f32[128,512]{1,0:T(8,128)}, f32[128,512]{1,0:T(8,128)}), (f32[128,512]{1,0:T(8,128)}, f32[128,512]{1,0:T(8,128)})) %all-reduce.15.cloned.1.call-update) | async-done | bytes 524304 | tf_op jit(solution)/shard_map/psum | solution.py:16
  1727.1 13.0 fusion.12
  1740.1 10.5 fusion.10
  (315 shorter events, 484.8 us)
Async XLA Ops:
  7.2 7.0 copy-start.1
  7.2 736.4 %all-reduce.17.cloned.1.call-start = ((), (), s32[]{:S(2)}) async-start(), calls=%async_computation.6 | async-start | bytes 393216 | tf_op jit(solution)/shard_map/psum | solution.py:16
  9.5 1.3 copy-start.9
  11.5 835.5 %all-gather.3.cloned.1.call-start = ((), (), s32[]{:S(2)}) async-start(), calls=%async_computation | async-start | bytes 10485760 | tf_op jit(solution)/shard_map/all_gather | solution.py:87
  95.4 650.9 %copy-start.13 = (f32[4096]{0:T(1024)S(1)}, f32[4096]{0:T(1024)}, u32[]{:S(2)}) copy-start(f32[4096]{0:T(1024)} %param.14) | copy-start | bytes 49156
  756.4 2.6 copy-start.6
  760.6 336.7 %all-reduce.9.cloned.1.call-start = ((), (), s32[]{:S(2)}) async-start(), calls=%async_computation.1 | async-start | bytes 2097152 | tf_op jit(solution)/shard_map/psum | solution.py:16
  850.1 11.7 copy-start.7
  946.1 0.7 copy-start.12
  991.2 240.5 %all-reduce.11.cloned.1.call-start = ((), (), s32[]{:S(2)}) async-start(), calls=%async_computation.2 | async-start | bytes 524288 | tf_op jit(solution)/shard_map/psum | solution.py:16
  1125.9 3.2 copy-start.2
  1129.3 353.4 %copy-start.3 = (f32[512,512]{1,0:T(8,128)}, f32[512,512]{1,0:T(8,128)S(1)}, u32[]{:S(2)}) copy-start(f32[512,512]{1,0:T(8,128)S(1)} %slice_select_fusion.1) | copy-start | bytes 3145732
  1130.3 198.0 %all-gather.5.cloned.1.call-start = ((), (), s32[]{:S(2)}) async-start(), calls=%async_computation.3 | async-start | bytes 10485760 | tf_op jit(solution)/shard_map/all_gather | solution.py:87
  1245.6 343.1 %all-reduce.13.cloned.1.call-start = ((), (), s32[]{:S(2)}) async-start(), calls=%async_computation.4 | async-start | bytes 2097152 | tf_op jit(solution)/shard_map/psum | solution.py:16
  1333.5 1.0 copy-start.8
  1434.9 0.7 copy-start.11
  1482.6 244.4 %all-reduce.15.cloned.1.call-start = ((), (), s32[]{:S(2)}) async-start(), calls=%async_computation.5 | async-start | bytes 1048576 | tf_op jit(solution)/shard_map/psum | solution.py:16
  1617.7 1.7 copy-start.4
  1618.6 3.0 copy-start
  1623.2 116.8 %slice-start = ((s8[7340032]{0:T(1024)(128)(4,1)}), s8[3145728]{0:T(1024)(128)(4,1)S(1)}, s32[]{:S(2)}) async-start(s8[7340032]{0:T(1024)(128)(4,1)} %bitcast.160), calls=%async_computation.7 | async-start | bytes 6291456
  1727.0 13.0 slice-start.1
  1727.0 13.0 copy-start.5
  1727.1 13.0 copy-start.10
Sparse Core Ops, SparseCore 0:
  12.2 103.4 all-reduce.16
  760.7 86.2 all-gather.2
  991.3 105.9 all-reduce.8
  1130.4 101.2 all-reduce.10
  1245.7 82.5 all-gather.4
  1482.8 105.9 all-reduce.12
  1623.3 103.6 all-reduce.14
where the time goes:
time: 1770 us; the launch traced here: 1760 us
  other arithmetic  985 us (56%)
  waiting for transfers between devices  571 us (32%)
  matrix products  125 us (7%)
  local copies, waits for them, and re-layouts  57.3 us (3%)
  between operations  20.1 us (1%)
    psum x5, waiting for transfers between devices, spread(): return lax.psum(jnp.where(mine, value, jnp.zeros_like(value)), axis)  402 us
    reduce_sum x35, other arithmetic, lookup_block(): jnp.sum(jnp.where(won_mask, losing[None, :], jnp.int32(0)), axis=1)  352 us
    reduce_sum x32, other arithmetic, lookup_block(): jnp.sum(jnp.where(won_mask, weights[None, :], jnp.float32(0.0)), axis=1)  322 us
    all_gather x2, waiting for transfers between devices, per_device(): gathered = lax.all_gather(current, 'col', axis=1, tiled=True)  168 us
    another operation x30, other arithmetic, per_device(): lowest = jnp.linalg.cholesky(gathered[:PANEL])  159 us
    another operation x5, other arithmetic, per_device(): inverse = jax.scipy.linalg.solve_triangular(lowest, identity, lower=True)  81.5 us
    dot_general x2, matrix products, per_device(): jnp.einsum('rk,jk->rj', gathered, inverse, precision=lax.Precision.HIGHEST)  57.4 us
    reduce_sum x3, other arithmetic, lookup_block(): jnp.sum(jnp.where(lost_mask, weights[None, :], jnp.float32(0.0)), axis=1)  50.6 us
  transfers between devices with their start and end apart: 7, of which 6 were waited for; matrix products, arithmetic and copies ran while one was open for 42% of the time, Pallas kernels for 0%

commit v1 on v0

v1 whole, which is shorter than its diff:
```python
import jax
import jax.numpy as jnp
from jax import lax
from jax.experimental import pallas as pl
from jax.experimental.pallas import tpu as pltpu
from jax.sharding import PartitionSpec as P

PANEL = 512
ROWS_DEV = 4096
CONFIGS = 131072
BLOCK = 128
WINDOW = 12
CHAIN = 2 * PANEL
COLUMNS = CHAIN + BLOCK
ROW_STEP = 512
LOG2E = 1.4426950408889634
VMEM_BYTES = 56 * 1024 * 1024
HIGHEST = lax.Precision.HIGHEST
f32, bf16, i32 = jnp.float32, jnp.bfloat16, jnp.int32


def iota(shape, dim):
    return lax.broadcasted_iota(i32, shape, dim)


def dot_nt(left, right, precision=None):
    return lax.dot_general(
        left, right, (((1,), (1,)), ((), ())), precision=precision, preferred_element_type=f32
    )


def dot_nn(left, right, precision=None):
    return lax.dot_general(
        left, right, (((1,), (0,)), ((), ())), precision=precision, preferred_element_type=f32
    )


def split3(value):
    high = value.astype(bf16)
    rest = value - high.astype(f32)
    middle = rest.astype(bf16)
    low = (rest - middle.astype(f32)).astype(bf16)
    return high, middle, low


def split2(value):
    high = value.astype(bf16)
    return high, (value - high.astype(f32)).astype(bf16)


TABLE_CHUNK = 2048


def tables_kernel(pairs_ref, weights_ref, offc_ref, cc_ref, offr_ref, cr_ref, wl_ref, acc_ref):
    row = iota((40, 1), 0)
    code = row + 20 * ((row >= 12).astype(i32) + (row >= 24).astype(i32))
    code = jnp.where(row < 36, code, -1)
    low_id = iota((BLOCK, 1), 0)
    acc_ref[...] = jnp.zeros_like(acc_ref)

    def step(index, carry):
        span = pl.ds(pl.multiple_of(index * TABLE_CHUNK, TABLE_CHUNK), TABLE_CHUNK)
        winner = pairs_ref[0:1, span]
        loser = pairs_ref[1:2, span]
        weight = weights_ref[0:1, span]
        place = (winner + 1024) & (CONFIGS - 1)
        offset = (loser - winner) & (CONFIGS - 1)
        one_hot = jnp.where(low_id == (place & 127), f32(1.0), f32(0.0)).astype(bf16)
        hit = code == (place >> 7)
        parts = [(offset >> 5).astype(f32), (offset & 31).astype(f32)]
        parts += [part.astype(f32) for part in split3(weight)]
        values = [jnp.where(hit, part, f32(0.0)) for part in parts]
        values.append(jnp.zeros((8, TABLE_CHUNK), f32))
        acc_ref[:, 0:208] += dot_nt(one_hot, jnp.concatenate(values, 0).astype(bf16))
        return carry

    lax.fori_loop(0, CONFIGS // TABLE_CHUNK, step, 0)
    turned = acc_ref[...].T
    offr = (turned[0:40] * 32.0 + turned[40:80]).astype(i32)
    cr = turned[80:120] + turned[120:160] + turned[160:200]
    offr_ref[...] = offr
    cr_ref[...] = cr
    offc = jnp.concatenate([offr, jnp.zeros((88, BLOCK), i32)], 0).T
    cc = jnp.concatenate([cr, jnp.zeros((88, BLOCK), f32)], 0).T
    offc_ref[...] = offc
    cc_ref[...] = cc
    place = iota((BLOCK, 1), 0)
    lane = iota((BLOCK, BLOCK), 1)
    rows = []
    for panel in range(3):
        lost = [jnp.zeros((1, BLOCK), f32) for _ in range(4)]
        for h in range(12):
            r = panel * WINDOW + h
            target = jnp.broadcast_to(offc[:, r : r + 1] + (place + BLOCK * (h - 8)), (BLOCK, BLOCK)) - lane
            weight = jnp.broadcast_to(cc[:, r : r + 1], (BLOCK, BLOCK))
            for d in range(4):
                if h - 8 <= d:
                    found = jnp.where(target == BLOCK * d, weight, f32(0.0))
                    lost[d] = lost[d] + jnp.sum(found, axis=0, keepdims=True)
        for d in range(4):
            r = panel * WINDOW + 8 + d
            rows.append(lost[d] + cr[r : r + 1])
    rows.append(jnp.zeros((4, BLOCK), f32))
    wl_ref[...] = jnp.concatenate(rows, 0)


def pair_tables(pairs, weights):
    return pl.pallas_call(
        tables_kernel,
        name="pair_tables",
        out_shape=(
            jax.ShapeDtypeStruct((BLOCK, BLOCK), i32),
            jax.ShapeDtypeStruct((BLOCK, BLOCK), f32),
            jax.ShapeDtypeStruct((40, BLOCK), i32),
            jax.ShapeDtypeStruct((40, BLOCK), f32),
            jax.ShapeDtypeStruct((16, BLOCK), f32),
        ),
        scratch_shapes=[pltpu.VMEM((BLOCK, 256), f32)],
        compiler_params=pltpu.CompilerParams(vmem_limit_bytes=VMEM_BYTES),
        cost_estimate=pl.CostEstimate(
            flops=2 * CONFIGS * BLOCK * 256, bytes_accessed=12 * CONFIGS, transcendentals=0
        ),
    )(pairs, weights)


def hessian_block(first_row, first_col, own, partner, diagonal):
    row = iota((BLOCK, BLOCK), 0) + first_row
    col = iota((BLOCK, BLOCK), 1) + first_col
    own_offset, own_weight = own
    partner_offset, partner_weight = partner
    value = jnp.where(row + own_offset == col, -own_weight, f32(0.0))
    value = value + jnp.where(col + partner_offset == row, -partner_weight, f32(0.0))
    return value + jnp.where(row == col, diagonal, f32(0.0))


def factor_tiles(tiles):
    tiles = list(tiles)
    count = len(tiles)
    sub = iota((8, BLOCK), 0)
    lane = iota((8, BLOCK), 1)
    for k in range(count):
        base = 8 * k
        inside = (lane >= base) & (lane < base + 8)
        eye = jnp.where(lane == sub + base, f32(1.0), f32(0.0))
        cols = [jnp.broadcast_to(tiles[k][:, base + j : base + j + 1], (8, BLOCK)) for j in range(8)]
        entry = {}
        for j in range(8):
            for i in range(j, 8):
                entry[i, j] = jnp.broadcast_to(cols[j][i : i + 1, :], (8, BLOCK))
        own = jnp.where(inside, eye, tiles[k])
        inverse = []
        for j in range(8):
            scale = 1.0 / entry[j, j]
            inverse.append(scale)
            ratio = {i: entry[i, j] * scale for i in range(j + 1, 8)}
            for i in range(j + 1, 8):
                for m in range(j + 1, i + 1):
                    entry[i, m] = entry[i, m] - ratio[i] * entry[m, j]
            if j < 7:
                step = jnp.where(sub > j, cols[j] * scale, f32(0.0))
                for m in range(j + 1, 8):
                    cols[m] = cols[m] - step * entry[m, j]
                own = own - step * jnp.broadcast_to(own[j : j + 1, :], (8, BLOCK))
        rows = [jnp.broadcast_to(own[j : j + 1, :], (8, BLOCK)) for j in range(8)]
        for t in range(k + 1, count):
            tile = tiles[t]
            left = [jnp.broadcast_to(tile[:, base + j : base + j + 1], (8, BLOCK)) for j in range(8)]
            tile = jnp.where(inside, f32(0.0), tile)
            for j in range(8):
                step = left[j] * inverse[j]
                for m in range(j + 1, 8):
                    left[m] = left[m] - step * entry[m, j]
                tile = tile - step * rows[j]
            tiles[t] = tile
        scale = inverse[0]
        for j in range(1, 8):
            scale = jnp.where(sub == j, inverse[j], scale)
        tiles[k] = own * jnp.sqrt(scale)
    return tiles


def chain_kernel(
    rank_ref, g0_ref, g1_ref, g2_ref, g3_ref, p2_ref, inv_ref, offc_ref, cc_ref, offr_ref, cr_ref, wl_ref,
    mhi_ref, mlo_ref, b6_ref, csq_ref, dg_ref, x_ref, pts_ref, lower_ref,
):
    c = rank_ref[1]
    inv = inv_ref[...]
    dg_ref[...] = wl_ref[...]
    for k, g_ref in enumerate((g0_ref, g1_ref, g2_ref, g3_ref)):
        place = (c + k) & 3
        for panel in range(2):
            rows = pl.ds(pl.multiple_of(panel * PANEL + place * BLOCK, BLOCK), BLOCK)
            pts_ref[rows, :] = g_ref[panel * 136 : panel * 136 + BLOCK, :] * inv
            line = pl.ds(panel * 4 + place, 1)
            dg_ref[line, :] += g_ref[panel * 136 + BLOCK : panel * 136 + BLOCK + 1, :]
    pts_ref[CHAIN:COLUMNS, :] = p2_ref[0:BLOCK, :] * inv
    dg_ref[pl.ds(8 + c, 1), :] += p2_ref[BLOCK : BLOCK + 1, :]

    points = pts_ref[...]
    csq_ref[...] = 1.0 - (0.5 * LOG2E) * dot_nt(jnp.ones((8, BLOCK), f32), points * points, HIGHEST)
    bh, bm, bl = split3(points * LOG2E)
    b6_ref[...] = jnp.concatenate([bh, bm, bh, bm, bl, bh], 1)
    for k in range(8):
        rows = slice(k * BLOCK, (k + 1) * BLOCK)
        own = pts_ref[rows, :]
        own_sq = (-0.5 * LOG2E) * jnp.sum(own * own, axis=1, keepdims=True)
        ah, am, al = split3(own)
        inner = dot_nt(jnp.concatenate([ah, ah, am, am, ah, al], 1), b6_ref[k * BLOCK :, :])
        x_ref[rows, k * BLOCK :] = jnp.exp2(inner + (own_sq + csq_ref[0:1, k * BLOCK :]))
        if k:
            x_ref[rows, : k * BLOCK] = jnp.zeros((BLOCK, k * BLOCK), f32)
    for panel in range(2):
        for b in range(4):
            r = panel * WINDOW + 8 + b
            for d in range(b, 4):
                s = panel * WINDOW + 8 + d
                at = (
                    slice(panel * PANEL + b * BLOCK, panel * PANEL + (b + 1) * BLOCK),
                    slice(panel * PANEL + d * BLOCK, panel * PANEL + (d + 1) * BLOCK),
                )
                line = panel * 4 + d
                x_ref[at] += hessian_block(
                    b * BLOCK, d * BLOCK,
                    (offc_ref[:, r : r + 1], cc_ref[:, r : r + 1]),
                    (offr_ref[s : s + 1, :], cr_ref[s : s + 1, :]),
                    dg_ref[line : line + 1, :],
                )

    sub = iota((8, BLOCK), 0)
    lane = iota((8, BLOCK), 1)
    chunk = 384

    def panel_step(k, carry):
        first = pl.multiple_of(k * BLOCK, BLOCK)
        own = pl.ds(first, BLOCK)
        tiles = [x_ref[pl.ds(pl.multiple_of(first + 8 * t, 8), 8), own] for t in range(16)]
        for t, tile in enumerate(factor_tiles(tiles)):
            lower_ref[8 * t : 8 * t + 8, :] = jnp.where(lane <= sub + 8 * t, tile, f32(0.0))
            x_ref[pl.ds(pl.multiple_of(first + 8 * t, 8), 8), own] = jnp.where(
                lane == sub + 8 * t, f32(1.0), f32(0.0)
            )
        lower = lower_ref[...]
        for n in range(0, COLUMNS, chunk):
            x_ref[own, n : n + chunk] = dot_nn(lower, x_ref[own, n : n + chunk], HIGHEST)

        def trailing(i, inner_carry):
            rows = pl.ds(pl.multiple_of(i * BLOCK, BLOCK), BLOCK)
            turned = x_ref[own, rows].T
            x_ref[rows, own] = jnp.zeros((BLOCK, BLOCK), f32)
            for n in range(0, COLUMNS, chunk):
                x_ref[rows, n : n + chunk] -= dot_nn(turned, x_ref[own, n : n + chunk], HIGHEST)
            return inner_carry

        lax.fori_loop(k + 1, 8, trailing, 0)
        return carry

    lax.fori_loop(0, 8, panel_step, 0)

    wide = iota((BLOCK, CHAIN), 1)
    for panel in range(2):
        rows = pl.ds(pl.multiple_of(panel * PANEL + c * BLOCK, BLOCK), BLOCK)
        value = jnp.where(wide < panel * PANEL + (c + 1) * BLOCK, x_ref[rows, :CHAIN], f32(0.0))
        high, low = split2(value)
        mhi_ref[panel * BLOCK : (panel + 1) * BLOCK, :] = high
        mlo_ref[panel * BLOCK : (panel + 1) * BLOCK, :] = low
    turned = [x_ref[i * BLOCK : (i + 1) * BLOCK, CHAIN:].T for i in range(8)]
    for n in range(8):
        cols = slice(n * BLOCK, (n + 1) * BLOCK)
        value = jnp.zeros((BLOCK, BLOCK), f32)
        for i in range(n, 8):
            value = value - dot_nn(turned[i], x_ref[i * BLOCK : (i + 1) * BLOCK, cols], HIGHEST)
        high, low = split2(value)
        mhi_ref[2 * BLOCK :, cols] = high
        mlo_ref[2 * BLOCK :, cols] = low


def panel_chain(rank, gathered, third, inv_length, tables):
    vmem = pl.BlockSpec(memory_space=pltpu.VMEM)
    return pl.pallas_call(
        chain_kernel,
        name="panel_chain",
        in_specs=[pl.BlockSpec(memory_space=pltpu.SMEM)] + [vmem] * 11,
        out_shape=(
            jax.ShapeDtypeStruct((3 * BLOCK, CHAIN), bf16),
            jax.ShapeDtypeStruct((3 * BLOCK, CHAIN), bf16),
            jax.ShapeDtypeStruct((COLUMNS, 6 * BLOCK), bf16),
            jax.ShapeDtypeStruct((8, COLUMNS), f32),
            jax.ShapeDtypeStruct((16, BLOCK), f32),
        ),
        scratch_shapes=[
            pltpu.VMEM((CHAIN, COLUMNS), f32),
            pltpu.VMEM((COLUMNS, BLOCK), f32),
            pltpu.VMEM((BLOCK, BLOCK), f32),
        ],
        compiler_params=pltpu.CompilerParams(vmem_limit_bytes=VMEM_BYTES),
        cost_estimate=pl.CostEstimate(
            flops=8 * CHAIN * CHAIN * CHAIN, bytes_accessed=8 * 1024 * 1024, transcendentals=CHAIN * COLUMNS
        ),
    )(rank, *gathered, third, inv_length, *tables)


def rows_kernel(
    rank_ref, feat_ref, inv_ref, mhi_ref, mlo_ref, b6_ref, csq_ref, dg_ref, offc_ref, cc_ref, offr_ref, cr_ref,
    factor_ref, schur_ref, s_ref,
):
    r_rank = rank_ref[0]
    c = rank_ref[1]
    n = pl.program_id(0)
    own = feat_ref[...] * inv_ref[...]
    own_sq = (-0.5 * LOG2E) * jnp.sum(own * own, axis=1, keepdims=True)
    ah, am, al = split3(own)
    a6 = jnp.concatenate([ah, ah, am, am, ah, al], 1)
    for first in range(0, COLUMNS, 384):
        inner = dot_nt(a6, b6_ref[first : first + 384, :])
        s_ref[:, first : first + 384] = jnp.exp2(inner + (own_sq + csq_ref[0:1, first : first + 384]))

    def add_hessian(panel, start):
        lane = iota((BLOCK, BLOCK), 1)

        def per_row(b, carry):
            first_row = start + b * BLOCK
            r = panel * WINDOW + 8 + (start // BLOCK) + b
            pick = lane == r
            own_offset = jnp.sum(jnp.where(pick, offc_ref[...], 0), axis=1, keepdims=True)
            own_weight = jnp.sum(jnp.where(pick, cc_ref[...], f32(0.0)), axis=1, keepdims=True)
            own_weight = jnp.where(first_row < PANEL, own_weight, f32(0.0))

            def per_col(d, inner_carry):
                which = jnp.where(panel == 2, c, d)
                s = panel * WINDOW + 8 + which
                partner_weight = jnp.where(first_row >= 0, cr_ref[pl.ds(s, 1), :], f32(0.0))
                value = hessian_block(
                    first_row, which * BLOCK, (own_offset, own_weight),
                    (offr_ref[pl.ds(s, 1), :], partner_weight), dg_ref[pl.ds(panel * 4 + which, 1), :],
                )
                rows = pl.ds(pl.multiple_of(b * BLOCK, BLOCK), BLOCK)
                cols = pl.ds(pl.multiple_of(panel * PANEL + d * BLOCK, BLOCK), BLOCK)
                s_ref[rows, cols] += value
                return inner_carry

            lax.fori_loop(0, jnp.where(panel == 2, 1, 4), per_col, 0)
            return carry

        lax.fori_loop(0, ROW_STEP // BLOCK, per_row, 0)

    @pl.when((r_rank <= 2) & (n <= 2))
    def _():
        add_hessian(r_rank, n * ROW_STEP)

    following = jnp.where(r_rank == 31, 0, r_rank + 1)

    @pl.when((following <= 2) & (n >= 6))
    def _():
        add_hessian(following, (n - 8) * ROW_STEP)

    first_hi, first_lo = split2(s_ref[:, :PANEL])
    second_hi, second_lo = split2(s_ref[:, PANEL:CHAIN])

    def product(first_row, last_row, left, first_col):
        hi, lo = left
        cols = slice(first_col, first_col + PANEL)
        rows = slice(first_row, last_row)
        return (
            dot_nt(hi, mhi_ref[rows, cols]) + dot_nt(lo, mhi_ref[rows, cols]) + dot_nt(hi, mlo_ref[rows, cols])
        )

    from_first = product(0, 3 * BLOCK, (first_hi, first_lo), 0)
    from_second = product(BLOCK, 3 * BLOCK, (second_hi, second_lo), PANEL)
    keep_second = jnp.where((r_rank == 0) & (n == 0), f32(0.0), f32(1.0))
    keep_schur = jnp.where((r_rank <= 1) & (n == 0), f32(0.0), f32(1.0))
    factor_ref[0] = from_first[:, :BLOCK]
    factor_ref[1] = (from_first[:, BLOCK : 2 * BLOCK] + from_second[:, :BLOCK]) * keep_second
    schur_ref[...] = (s_ref[:, CHAIN:] + from_first[:, 2 * BLOCK :] + from_second[:, BLOCK:]) * keep_schur


def own_rows(rank, features, inv_length, chain, tables):
    def whole(shape):
        return pl.BlockSpec(shape, lambda n: (0, 0))

    offc, cc, offr, cr, _ = tables
    return pl.pallas_call(
        rows_kernel,
        name="own_rows",
        grid=(ROWS_DEV // ROW_STEP,),
        in_specs=[
            pl.BlockSpec(memory_space=pltpu.SMEM),
            pl.BlockSpec((ROW_STEP, BLOCK), lambda n: (n, 0)),
            whole((1, BLOCK)),
            whole((3 * BLOCK, CHAIN)),
            whole((3 * BLOCK, CHAIN)),
            whole((COLUMNS, 6 * BLOCK)),
            whole((8, COLUMNS)),
            whole((16, BLOCK)),
            whole((BLOCK, BLOCK)),
            whole((BLOCK, BLOCK)),
            whole((40, BLOCK)),
            whole((40, BLOCK)),
        ],
        out_specs=(
            pl.BlockSpec((2, ROW_STEP, BLOCK), lambda n: (0, n, 0)),
            pl.BlockSpec((ROW_STEP, BLOCK), lambda n: (n, 0)),
        ),
        out_shape=(
            jax.ShapeDtypeStruct((2, ROWS_DEV, BLOCK), f32),
            jax.ShapeDtypeStruct((ROWS_DEV, BLOCK), f32),
        ),
        scratch_shapes=[pltpu.VMEM((ROW_STEP, COLUMNS), f32)],
        compiler_params=pltpu.CompilerParams(vmem_limit_bytes=VMEM_BYTES),
        cost_estimate=pl.CostEstimate(
            flops=2 * ROWS_DEV * COLUMNS * 768 + 6 * ROWS_DEV * CHAIN * 384,
            bytes_accessed=12 * 1024 * 1024,
            transcendentals=ROWS_DEV * COLUMNS,
        ),
    )(rank, features, inv_length, *chain, offc, cc, offr, cr)


def row_index(z, y, core):
    return (z % 4) * 8 + (y % 4) * 2 + core


def share_panels(features, nugget):
    row = lax.axis_index("row")
    col = lax.axis_index("col")
    z, y, core = row // 8, (row // 2) % 4, row % 2
    quarter = lax.dynamic_slice_in_dim(features, col * BLOCK, BLOCK, 0)
    extra = lax.dynamic_slice_in_dim(nugget, col * BLOCK, BLOCK, 0)[None, :]
    mine = jnp.concatenate([quarter, jnp.broadcast_to(extra, (8, BLOCK))], 0)

    def send(value, pairs):
        return lax.ppermute(value, "row", pairs)

    along_z = [
        send(mine, [(row_index(0, *at), row_index(k, *at)) for at in ((0, 0), (0, 1), (1, 0))]) for k in (1, 2, 3)
    ]
    for k in (1, 2, 3):
        mine = jnp.where(z == k, along_z[k - 1], mine)
    along_y = [
        send(
            mine,
            [
                (row_index(k, at, half), row_index(k, at + s, half))
                for k in range(4)
                for at, half in ((0, 0), (0, 1), (1, 0))
            ],
        )
        for s in (1, 2, 3)
    ]
    first, third = mine, mine
    for s in (1, 2, 3):
        first = jnp.where(y == s, along_y[s - 1], first)
        third = jnp.where(y == (1 + s) % 4, along_y[s - 1], third)
    other = send(jnp.concatenate([first, third], 0), [(i, i ^ 1) for i in range(32)])
    low = core == 0
    pair = jnp.concatenate([jnp.where(low, first, other[:136]), jnp.where(low, other[:136], first)], 0)
    third = jnp.where(low, third, other[136:])
    gathered = [pair] + [lax.ppermute(pair, "col", [((i + k) % 4, i) for i in range(4)]) for k in (1, 2, 3)]
    return gathered, third


def per_device(features, inv_length, nugget, pairs, weights):
    rank = jnp.stack([lax.axis_index("row"), lax.axis_index("col")]).astype(i32)
    inv_length = inv_length.reshape(1, BLOCK)
    gathered, third = share_panels(features, nugget)
    tables = pair_tables(pairs, weights.reshape(1, CONFIGS))
    chain = panel_chain(rank, gathered, third, inv_length, tables)
    return own_rows(rank, features, inv_length, chain, tables)


def solution(mesh):
    placed = (P("row", None), P(), P("row"), P(), P())
    return jax.shard_map(
        per_device,
        mesh=mesh,
        in_specs=placed,
        out_specs=(P(None, "row", "col"), P("row", "col")),
        check_vma=False,
    )
```

time: 1770 us -> 181 us (0.10)
  other arithmetic: 985 us -> 1.33 us
  waiting for transfers between devices: 571 us -> 3.63 us
  Pallas kernels: 0 us -> 148 us
  matrix products: 125 us -> 0 us
  local copies, waits for them, and re-layouts: 57.3 us -> 2.33 us
  starting transfers between devices: 1.21 us -> 24.4 us
  between operations: 20.1 us -> 0.82 us
    reduce_sum x72 -> x0, other arithmetic: 728 us -> none  [the longest x35 352 us: lookup_block(): jnp.sum(jnp.where(won_mask, losing[None, :], jnp.int32(0)), axis=1)]
    psum x5 -> x0, waiting for transfers between devices: 402 us -> none  [spread(): return lax.psum(jnp.where(mine, value, jnp.zeros_like(value)), axis)]
    another operation x40 -> x1, other arithmetic: 250 us -> 0.62 us  [per_device(): rank = jnp.stack([lax.axis_index('row'), lax.axis_index('col')]).astype(i32)]
    all_gather x2 -> x0, waiting for transfers between devices: 168 us -> none  [per_device(): gathered = lax.all_gather(current, 'col', axis=1, tiled=True)]
    pallas_call x0 -> x3, Pallas kernels: none -> 148 us  [the longest x1 80.5 us: panel_chain(): pl.pallas_call(chain_kernel, name='panel_chain', in_specs=[pl.BlockSpec(m...]
    dot_general x6 -> x0, matrix products: 105 us -> none  [the longest x2 57.4 us: per_device(): jnp.einsum('rk,jk->rj', gathered, inverse, precision=lax.Precision.HIGHEST)]
    ppermute x0 -> x10, starting transfers between devices: none -> 24.4 us  [the longest x7 19.5 us: send(): return lax.ppermute(value, 'row', pairs)]
    another operation x35 -> x0, local copies, waits for them, and re-layouts: 19.9 us -> none  [the longest x27 19.6 us: per_device(): inverse = jax.scipy.linalg.solve_triangular(lowest, identity, lower=True)]
  transfers between devices with their start and end apart: 7 -> 10, of which waited for: 6 -> 3; matrix products, arithmetic and copies ran while one was open for 42% -> 0% of each run, Pallas kernels for 0% -> 18%
where the time goes in v1:
time: 181 us; the launch traced here: 180 us
  Pallas kernels  148 us (82%)
  starting transfers between devices  24.4 us (13%)
  waiting for transfers between devices  3.63 us (2%)
  local copies, waits for them, and re-layouts  2.33 us (1%)
    pallas_call x1, Pallas kernels, panel_chain(): pl.pallas_call(chain_kernel, name='panel_chain', in_specs=[pl.BlockSpec(m...  80.5 us
    pallas_call x1, Pallas kernels, own_rows(): pl.pallas_call(rows_kernel, name='own_rows', grid=(ROWS_DEV // ROW_STEP,)...  35.2 us
    pallas_call x1, Pallas kernels, pair_tables(): pl.pallas_call(tables_kernel, name='pair_tables', out_shape=(jax.ShapeDty...  32.3 us
    ppermute x7, starting transfers between devices, send(): return lax.ppermute(value, 'row', pairs)  19.5 us
    ppermute x3, starting transfers between devices, share_panels(): lax.ppermute(pair, 'col', [((i + k) % 4, i) for i in range(4)])  4.88 us
  transfers between devices with their start and end apart: 10, of which 3 were waited for; matrix products, arithmetic and copies ran while one was open for 0% of the time, Pallas kernels for 18%

profile of v1, /device:TPU:1, one launch (start us, length us, event | category | flops | bytes accessed | tf_op | source)
XLA Modules:
  0.0 180.4 jit_solution(4100198682564029435)
XLA Ops:
  0.6 0.8 dynamic_slice.7
  1.4 0.8 constant_dynamic-slice_fusion
  2.3 4.4 %collective-permute-start.2 = (f32[136,128]{1,0:T(8,128)S(1)}, f32[136,128]{1,0:T(8,128)S(1)}, u32[]{:S(2)}, u32[]{:S(2)}) collective-permute-start(f32[136,128]{1,0:T(8,128)S(1)} %pad_maximum_fusion.2), channel_id=1, source_target_pairs={{0,32},{4,36},{8,40},{1,33},{5,37},{9,41},{2,34},{6,38},{10,42},{3... | collective-permute-start | bytes 208904 | tf_op jit(solution)/shard_map/ppermute | solution.py:430
  6.6 2.6 %collective-permute-start.1 = (f32[136,128]{1,0:T(8,128)S(1)}, f32[136,128]{1,0:T(8,128)S(1)}, u32[]{:S(2)}, u32[]{:S(2)}) collective-permute-start(f32[136,128]{1,0:T(8,128)S(1)} %pad_maximum_fusion.2), channel_id=1, source_target_pairs={{0,64},{4,68},{8,72},{1,65},{5,69},{9,73},{2,66},{6,70},{10,74},{3... | collective-permute-start | bytes 208904 | tf_op jit(solution)/shard_map/ppermute | solution.py:430
  9.3 1.3 collective-permute-start
  10.6 0.0 collective-permute-done.2
  10.6 0.0 collective-permute-done.1
  10.6 1.3 collective-permute-done
  11.9 1.3 collective-permute-start.5
  13.2 1.3 collective-permute-start.4
  14.5 1.3 collective-permute-start.3
  15.9 0.0 collective-permute-done.5
  15.9 0.0 collective-permute-done.4
  15.9 1.3 collective-permute-done.3
  17.2 7.4 %collective-permute-start.6 = (f32[272,128]{1,0:T(8,128)S(1)}, f32[272,128]{1,0:T(8,128)S(1)}, u32[]{:S(2)}, u32[]{:S(2)}) collective-permute-start(f32[272,128]{1,0:T(8,128)S(1)} %pad_maximum_fusion), channel_id=1, source_target_pairs={{0,4},{4,0},{8,12},{12,8},{16,20},{20,16},{24,28},{28,24},{32,36},... | collective-permute-start | bytes 417800 | tf_op jit(solution)/shard_map/ppermute | solution.py:430
  24.6 1.0 collective-permute-done.6
  25.6 0.6 slice_select_fusion.2
  26.2 0.0 copy-start
  26.3 1.3 collective-permute-start.9
  27.5 2.5 %collective-permute-start.8 = (f32[272,128]{1,0:T(8,128)S(1)}, f32[272,128]{1,0:T(8,128)S(1)}, u32[]{:S(2)}, u32[]{:S(2)}) collective-permute-start(f32[272,128]{1,0:T(8,128)S(1)} %pad_maximum_fusion.1.g0_ref), channel_id=1, source_target_pairs={{2,0},{3,1},{0,2},{1,3},{6,4},{7,5},{4,6},{5,7},{10,8},{11,9},{8,1... | collective-permute-start | bytes 417800 | tf_op jit(solution)/shard_map/ppermute | solution.py:456
  30.0 1.2 collective-permute-start.7
  31.1 32.3 %pair_tables.1 = (s32[128,128]{1,0:T(8,128)}, f32[128,128]{1,0:T(8,128)}, s32[40,128]{1,0:T(8,128)}, f32[40,128]{1,0:T(8,128)}, f32[16,128]{1,0:T(8,128)}) custom-call(s32[2,131072]{1,0:T(2,128)} %pairs_ref.1, f32[1,131072]{1,0:T(1,128)} %bitcast.4), custom_call_target="tpu_custom_call" | custom-call | flops 8589934592 | bytes 1572864 | tf_op jit(solution)/shard_map/pair_tables/pallas_call | solution.py:108
  63.4 0.0 copy-done
  63.4 0.6 pad_add_fusion.rank_ref
  64.0 0.0 collective-permute-done.9.g3_ref
  64.0 0.0 copy-start.1
  64.0 0.0 collective-permute-done.8.g2_ref
  64.0 0.0 copy-start.2
  64.1 0.0 collective-permute-done.7.g1_ref
  64.1 0.0 copy-start.3
  64.1 0.6 copy-done.1
  64.7 0.0 copy-done.2
  64.7 0.0 copy-done.3
  64.8 80.5 %panel_chain.1 = (bf16[384,1024]{1,0:T(8,128)(2,1)}, bf16[384,1024]{1,0:T(8,128)(2,1)}, bf16[1152,768]{1,0:T(8,128)(2,1)}, f32[8,1152]{1,0:T(8,128)}, f32[16,128]{1,0:T(8,128)}) custom-call(s32[2]{0:T(128)} %pad_add_fusion.rank_ref, f32[272,128]{1,0:T(8,128)} %copy-done, f32[272,128]{1,0:T(8,128)} %copy-done.3, f32[272,128]{1,0:T(8,128)} %copy-done.2, ...), custom_call_target="tpu_custom_call" | custom-call | flops 8589934592 | bytes 8388608 | tf_op jit(solution)/shard_map/panel_chain/pallas_call | solution.py:279
  145.3 35.2 %own_rows.1 = (f32[2,4096,128]{2,1,0:T(8,128)}, f32[4096,128]{1,0:T(8,128)}) custom-call(s32[2]{0:T(128)} %pad_add_fusion.rank_ref, f32[4096,128]{1,0:T(8,128)} %feat_ref.1, f32[1,128]{1,0:T(1,128)} %bitcast.6, bf16[384,1024]{1,0:T(8,128)(2,1)} %get-tuple-element.17.mhi_ref, bf16[384,1024]{1,0:T(8,128)(2,1)} %get-tuple-element.18.mlo_ref, ...), custom_call_target="tpu_custom_call" | custom-call | flops 16911433728 | bytes 12582912 | tf_op jit(solution)/shard_map/own_rows/pallas_call | solution.py:381
  (6 shorter events, 0.1 us)
Async XLA Ops:
  2.3 8.3 %collective-permute-start.2 = (f32[136,128]{1,0:T(8,128)S(1)}, f32[136,128]{1,0:T(8,128)S(1)}, u32[]{:S(2)}, u32[]{:S(2)}) collective-permute-start(f32[136,128]{1,0:T(8,128)S(1)} %pad_maximum_fusion.2), channel_id=1, source_target_pairs={{0,32},{4,36},{8,40},{1,33},{5,37},{9,41},{2,34},{6,38},{10,42},{3... | collective-permute-start | bytes 208904 | tf_op jit(solution)/shard_map/ppermute | solution.py:430
  6.6 4.0 %collective-permute-start.1 = (f32[136,128]{1,0:T(8,128)S(1)}, f32[136,128]{1,0:T(8,128)S(1)}, u32[]{:S(2)}, u32[]{:S(2)}) collective-permute-start(f32[136,128]{1,0:T(8,128)S(1)} %pad_maximum_fusion.2), channel_id=1, source_target_pairs={{0,64},{4,68},{8,72},{1,65},{5,69},{9,73},{2,66},{6,70},{10,74},{3... | collective-permute-start | bytes 208904 | tf_op jit(solution)/shard_map/ppermute | solution.py:430
  9.3 2.7 %collective-permute-start = (f32[136,128]{1,0:T(8,128)S(1)}, f32[136,128]{1,0:T(8,128)S(1)}, u32[]{:S(2)}, u32[]{:S(2)}) collective-permute-start(f32[136,128]{1,0:T(8,128)S(1)} %pad_maximum_fusion.2), channel_id=1, source_target_pairs={{0,96},{4,100},{8,104},{1,97},{5,101},{9,105},{2,98},{6,102},{10,1... | collective-permute-start | bytes 208904 | tf_op jit(solution)/shard_map/ppermute | solution.py:430
  11.9 3.9 %collective-permute-start.5 = (f32[136,128]{1,0:T(8,128)S(1)}, f32[136,128]{1,0:T(8,128)S(1)}, u32[]{:S(2)}, u32[]{:S(2)}) collective-permute-start(f32[136,128]{1,0:T(8,128)S(1)} %select_select_fusion.2), channel_id=1, source_target_pairs={{0,8},{4,12},{8,16},{32,40},{36,44},{40,48},{64,72},{68,76},{72,80... | collective-permute-start | bytes 208904 | tf_op jit(solution)/shard_map/ppermute | solution.py:430
  13.2 2.7 %collective-permute-start.4 = (f32[136,128]{1,0:T(8,128)S(1)}, f32[136,128]{1,0:T(8,128)S(1)}, u32[]{:S(2)}, u32[]{:S(2)}) collective-permute-start(f32[136,128]{1,0:T(8,128)S(1)} %select_select_fusion.2), channel_id=1, source_target_pairs={{0,16},{4,20},{8,24},{32,48},{36,52},{40,56},{64,80},{68,84},{72,8... | collective-permute-start | bytes 208904 | tf_op jit(solution)/shard_map/ppermute | solution.py:430
  14.5 2.7 %collective-permute-start.3 = (f32[136,128]{1,0:T(8,128)S(1)}, f32[136,128]{1,0:T(8,128)S(1)}, u32[]{:S(2)}, u32[]{:S(2)}) collective-permute-start(f32[136,128]{1,0:T(8,128)S(1)} %select_select_fusion.2), channel_id=1, source_target_pairs={{0,24},{4,28},{8,0},{32,56},{36,60},{40,32},{64,88},{68,92},{72,64... | collective-permute-start | bytes 208904 | tf_op jit(solution)/shard_map/ppermute | solution.py:430
  17.2 8.3 %collective-permute-start.6 = (f32[272,128]{1,0:T(8,128)S(1)}, f32[272,128]{1,0:T(8,128)S(1)}, u32[]{:S(2)}, u32[]{:S(2)}) collective-permute-start(f32[272,128]{1,0:T(8,128)S(1)} %pad_maximum_fusion), channel_id=1, source_target_pairs={{0,4},{4,0},{8,12},{12,8},{16,20},{20,16},{24,28},{28,24},{32,36},... | collective-permute-start | bytes 417800 | tf_op jit(solution)/shard_map/ppermute | solution.py:430
  26.2 37.2 %copy-start = (f32[272,128]{1,0:T(8,128)}, f32[272,128]{1,0:T(8,128)S(1)}, u32[]{:S(2)}) copy-start(f32[272,128]{1,0:T(8,128)S(1)} %pad_maximum_fusion.1.g0_ref) | copy-start | bytes 417796
  26.3 37.8 %collective-permute-start.9 = (f32[272,128]{1,0:T(8,128)S(1)}, f32[272,128]{1,0:T(8,128)S(1)}, u32[]{:S(2)}, u32[]{:S(2)}) collective-permute-start(f32[272,128]{1,0:T(8,128)S(1)} %pad_maximum_fusion.1.g0_ref), channel_id=1, source_target_pairs={{3,0},{0,1},{1,2},{2,3},{7,4},{4,5},{5,6},{6,7},{11,8},{8,9},{9,10... | collective-permute-start | bytes 417800 | tf_op jit(solution)/shard_map/ppermute | solution.py:456
  27.5 36.5 %collective-permute-start.8 = (f32[272,128]{1,0:T(8,128)S(1)}, f32[272,128]{1,0:T(8,128)S(1)}, u32[]{:S(2)}, u32[]{:S(2)}) collective-permute-start(f32[272,128]{1,0:T(8,128)S(1)} %pad_maximum_fusion.1.g0_ref), channel_id=1, source_target_pairs={{2,0},{3,1},{0,2},{1,3},{6,4},{7,5},{4,6},{5,7},{10,8},{11,9},{8,1... | collective-permute-start | bytes 417800 | tf_op jit(solution)/shard_map/ppermute | solution.py:456
  30.0 34.1 %collective-permute-start.7 = (f32[272,128]{1,0:T(8,128)S(1)}, f32[272,128]{1,0:T(8,128)S(1)}, u32[]{:S(2)}, u32[]{:S(2)}) collective-permute-start(f32[272,128]{1,0:T(8,128)S(1)} %pad_maximum_fusion.1.g0_ref), channel_id=1, source_target_pairs={{1,0},{2,1},{3,2},{0,3},{5,4},{6,5},{7,6},{4,7},{9,8},{10,9},{11,1... | collective-permute-start | bytes 417800 | tf_op jit(solution)/shard_map/ppermute | solution.py:456
  64.0 0.7 copy-start.1
  64.0 0.7 copy-start.2
  64.1 0.7 copy-start.3

commit v2 on v1

v2 whole, which is shorter than its diff:
```python
import jax
import jax.numpy as jnp
from jax import lax
from jax.experimental import pallas as pl
from jax.experimental.pallas import tpu as pltpu
from jax.sharding import PartitionSpec as P

PANEL = 512
ROWS_DEV = 4096
CONFIGS = 131072
BLOCK = 128
WINDOW = 12
CHAIN = 2 * PANEL
COLUMNS = CHAIN + BLOCK
ROW_STEP = 512
ROW_STEPS = ROWS_DEV // ROW_STEP
ROOT_LOG2E = 1.2011224087864498
VMEM_BYTES = 56 * 1024 * 1024
HIGHEST = lax.Precision.HIGHEST
f32, bf16, i32 = jnp.float32, jnp.bfloat16, jnp.int32


def iota(shape, dim):
    return lax.broadcasted_iota(i32, shape, dim)


def dot_nt(left, right, precision=None):
    return lax.dot_general(
        left, right, (((1,), (1,)), ((), ())), precision=precision, preferred_element_type=f32
    )


def dot_nn(left, right, precision=None):
    return lax.dot_general(
        left, right, (((1,), (0,)), ((), ())), precision=precision, preferred_element_type=f32
    )


def split3(value):
    high = value.astype(bf16)
    rest = value - high.astype(f32)
    middle = rest.astype(bf16)
    low = (rest - middle.astype(f32)).astype(bf16)
    return high, middle, low


def split2(value):
    high = value.astype(bf16)
    return high, (value - high.astype(f32)).astype(bf16)


TABLE_CHUNK = 2048
TABLE_ROWS = 96
QUARTER = BLOCK + 8


def tables_kernel(rank_ref, pairs_ref, weights_ref, out_ref, acc_ref):
    row = iota((40, 1), 0)
    code = row + 20 * ((row >= 12).astype(i32) + (row >= 24).astype(i32))
    code = jnp.where(row < 36, code, -1)
    low_id = iota((BLOCK, 1), 0)
    acc_ref[...] = jnp.zeros_like(acc_ref)
    share = CONFIGS // 8
    start = (2 * rank_ref[1] + (rank_ref[0] & 1)) * share

    def step(index, carry):
        span = pl.ds(pl.multiple_of(start + index * TABLE_CHUNK, TABLE_CHUNK), TABLE_CHUNK)
        winner = pairs_ref[0:1, span]
        loser = pairs_ref[1:2, span]
        weight = weights_ref[0:1, span]
        place = (winner + 1024) & (CONFIGS - 1)
        offset = (loser - winner) & (CONFIGS - 1)
        one_hot = jnp.where(low_id == (place & 127), f32(1.0), f32(0.0)).astype(bf16)
        hit = code == (place >> 7)
        parts = [(offset >> 5).astype(f32), (offset & 31).astype(f32)]
        parts += [part.astype(f32) for part in split3(weight)]
        values = [jnp.where(hit, part, f32(0.0)) for part in parts]
        values.append(jnp.zeros((8, TABLE_CHUNK), f32))
        acc_ref[:, 0:208] += dot_nt(one_hot, jnp.concatenate(values, 0).astype(bf16))
        return carry

    lax.fori_loop(0, share // TABLE_CHUNK, step, 0)
    turned = acc_ref[...].T
    offr = turned[0:40] * 32.0 + turned[40:80]
    cr = turned[80:120] + turned[120:160] + turned[160:200]
    out_ref[0:40, :] = offr
    out_ref[40:80, :] = cr
    offc = jnp.concatenate([offr.astype(i32), jnp.zeros((88, BLOCK), i32)], 0).T
    cc = jnp.concatenate([cr, jnp.zeros((88, BLOCK), f32)], 0).T
    place = iota((BLOCK, 1), 0)
    lane = iota((BLOCK, BLOCK), 1)
    rows = []
    for panel in range(3):
        lost = [jnp.zeros((1, BLOCK), f32) for _ in range(4)]
        for h in range(12):
            r = panel * WINDOW + h
            target = jnp.broadcast_to(offc[:, r : r + 1] + (place + BLOCK * (h - 8)), (BLOCK, BLOCK)) - lane
            weight = jnp.broadcast_to(cc[:, r : r + 1], (BLOCK, BLOCK))
            for d in range(4):
                if h - 8 <= d:
                    found = jnp.where(target == BLOCK * d, weight, f32(0.0))
                    lost[d] = lost[d] + jnp.sum(found, axis=0, keepdims=True)
        for d in range(4):
            r = panel * WINDOW + 8 + d
            rows.append(lost[d] + cr[r : r + 1])
    rows.append(jnp.zeros((4, BLOCK), f32))
    out_ref[80:96, :] = jnp.concatenate(rows, 0)


def pair_tables(rank, pairs, weights):
    vmem = pl.BlockSpec(memory_space=pltpu.VMEM)
    return pl.pallas_call(
        tables_kernel,
        name="pair_tables",
        in_specs=[pl.BlockSpec(memory_space=pltpu.SMEM), vmem, vmem],
        out_shape=jax.ShapeDtypeStruct((TABLE_ROWS, BLOCK), f32),
        scratch_shapes=[pltpu.VMEM((BLOCK, 256), f32)],
        compiler_params=pltpu.CompilerParams(vmem_limit_bytes=VMEM_BYTES),
        cost_estimate=pl.CostEstimate(
            flops=2 * CONFIGS * BLOCK * 256, bytes_accessed=12 * CONFIGS, transcendentals=0
        ),
    )(rank, pairs, weights)


def hessian_block(first_row, first_col, own, partner, diagonal):
    row = iota((BLOCK, BLOCK), 0) + first_row
    col = iota((BLOCK, BLOCK), 1) + first_col
    own_offset, own_weight = own
    partner_offset, partner_weight = partner
    value = jnp.where(row + own_offset == col, -own_weight, f32(0.0))
    value = value + jnp.where(col + partner_offset == row, -partner_weight, f32(0.0))
    return value + jnp.where(row == col, diagonal, f32(0.0))


def factor_tiles(tiles):
    tiles = list(tiles)
    count = len(tiles)
    sub = iota((8, BLOCK), 0)
    lane = iota((8, BLOCK), 1)
    for k in range(count):
        base = 8 * k
        inside = (lane >= base) & (lane < base + 8)
        eye = jnp.where(lane == sub + base, f32(1.0), f32(0.0))
        cols = [jnp.broadcast_to(tiles[k][:, base + j : base + j + 1], (8, BLOCK)) for j in range(8)]
        entry = {}
        for j in range(8):
            for i in range(j, 8):
                entry[i, j] = jnp.broadcast_to(cols[j][i : i + 1, :], (8, BLOCK))
        own = jnp.where(inside, eye, tiles[k])
        inverse = []
        for j in range(8):
            scale = 1.0 / entry[j, j]
            inverse.append(scale)
            ratio = {i: entry[i, j] * scale for i in range(j + 1, 8)}
            for i in range(j + 1, 8):
                for m in range(j + 1, i + 1):
                    entry[i, m] = entry[i, m] - ratio[i] * entry[m, j]
            if j < 7:
                step = jnp.where(sub > j, cols[j] * scale, f32(0.0))
                for m in range(j + 1, 8):
                    cols[m] = cols[m] - step * entry[m, j]
                own = own - step * jnp.broadcast_to(own[j : j + 1, :], (8, BLOCK))
        rows = [jnp.broadcast_to(own[j : j + 1, :], (8, BLOCK)) for j in range(8)]
        for t in range(k + 1, count):
            tile = tiles[t]
            left = [jnp.broadcast_to(tile[:, base + j : base + j + 1], (8, BLOCK)) for j in range(8)]
            tile = jnp.where(inside, f32(0.0), tile)
            for j in range(8):
                step = left[j] * inverse[j]
                for m in range(j + 1, 8):
                    left[m] = left[m] - step * entry[m, j]
                tile = tile - step * rows[j]
            tiles[t] = tile
        scale = inverse[0]
        for j in range(1, 8):
            scale = jnp.where(sub == j, inverse[j], scale)
        tiles[k] = own * jnp.sqrt(scale)
    return tiles


def dot3(left, right):
    lh, ll = left
    rh, rl = right
    return dot_nn(lh, rh) + (dot_nn(lh, rl) + dot_nn(ll, rh))


def points_parts(value, scale):
    high, middle = split2(value * scale)
    return high, middle, high.astype(f32) + middle.astype(f32)


def chain_kernel(
    rank_ref, mine_ref, other_ref, inv_ref, feat_ref, factor_hbm, schur_hbm,
    x_ref, dg_ref, offc_ref, cc_ref, offr_ref, cr_ref, b4_ref, csq_ref, pts_ref, t_ref, lower_ref, d_ref,
    wh_ref, wl_ref, uh_ref, ul_ref, sh_ref, sl_ref, s2_ref, mh_ref, ml_ref, out_ref, out_sem,
):
    r_rank = rank_ref[0]
    c = rank_ref[1]
    even = (r_rank & 1) == 0
    scale = inv_ref[...] * ROOT_LOG2E

    def of_panel(panel, rows):
        return jnp.where(even == (panel != 1), mine_ref[rows, :], other_ref[rows, :])

    at = slice(4 * QUARTER, 4 * QUARTER + TABLE_ROWS)
    table = mine_ref[at, :] + other_ref[at, :]
    offr = table[0:40].astype(i32)
    cr = table[40:80]
    offr_ref[...] = offr
    cr_ref[...] = cr
    offc_ref[...] = jnp.concatenate([offr, jnp.zeros((88, BLOCK), i32)], 0).T
    cc_ref[...] = jnp.concatenate([cr, jnp.zeros((88, BLOCK), f32)], 0).T
    dg_ref[...] = table[80:96]
    for k in range(4):
        place = (c + k) & 3
        first = k * QUARTER
        for panel in range(2):
            rows = pl.ds(pl.multiple_of(panel * PANEL + place * BLOCK, BLOCK), BLOCK)
            pts_ref[rows, :] = of_panel(panel, slice(first, first + BLOCK))
            dg_ref[pl.ds(panel * 4 + place, 1), :] += of_panel(panel, slice(first + BLOCK, first + BLOCK + 1))
    first = 4 * QUARTER + TABLE_ROWS
    pts_ref[CHAIN:COLUMNS, :] = of_panel(2, slice(first, first + BLOCK))
    dg_ref[pl.ds(8 + c, 1), :] += of_panel(2, slice(first + BLOCK, first + BLOCK + 1))

    for k in range(9):
        cols = slice(k * BLOCK, (k + 1) * BLOCK)
        high, middle, near = points_parts(pts_ref[cols, :], scale)
        near = near.T
        csq_ref[:, cols] = jnp.broadcast_to(1.0 - 0.5 * jnp.sum(near * near, axis=0, keepdims=True), (8, BLOCK))
        high, middle = split2(near)
        for n, part in enumerate((high, middle, high, middle)):
            b4_ref[n * BLOCK : (n + 1) * BLOCK, cols] = part

    def kernel_rows(value, cols):
        high, middle, near = points_parts(value, scale)
        own_sq = -0.5 * jnp.sum(near * near, axis=1, keepdims=True)
        inner = dot_nn(jnp.concatenate([high, high, middle, middle], 1), b4_ref[:, cols])
        return jnp.exp2(inner + (own_sq + csq_ref[0:1, cols]))

    for k in range(8):
        rows = slice(k * BLOCK, (k + 1) * BLOCK)
        x_ref[rows, k * BLOCK :] = kernel_rows(pts_ref[rows, :], slice(k * BLOCK, COLUMNS))
        if k:
            x_ref[rows, : k * BLOCK] = jnp.zeros((BLOCK, k * BLOCK), f32)
    for ref in (wh_ref, wl_ref, uh_ref, ul_ref, t_ref, lower_ref):
        ref[...] = jnp.zeros_like(ref)
    for panel in range(2):
        for b in range(4):
            r = panel * WINDOW + 8 + b
            for d in range(b, 4):
                s = panel * WINDOW + 8 + d
                at = (
                    slice(panel * PANEL + b * BLOCK, panel * PANEL + (b + 1) * BLOCK),
                    slice(panel * PANEL + d * BLOCK, panel * PANEL + (d + 1) * BLOCK),
                )
                line = panel * 4 + d
                x_ref[at] += hessian_block(
                    b * BLOCK, d * BLOCK,
                    (offc_ref[:, r : r + 1], cc_ref[:, r : r + 1]),
                    (offr_ref[s : s + 1, :], cr_ref[s : s + 1, :]),
                    dg_ref[line : line + 1, :],
                )

    sub = iota((8, BLOCK), 0)
    lane = iota((8, BLOCK), 1)
    d_ref[...] = x_ref[:BLOCK, :BLOCK]

    def block_rows(index):
        return pl.ds(pl.multiple_of(index * BLOCK, BLOCK), BLOCK)

    def finish_row(k):
        own = block_rows(k)
        row = dot3(split2(lower_ref[...]), split2(t_ref[...]))
        high, low = split2(row)
        wh_ref[:, own] = jnp.zeros((CHAIN, BLOCK), bf16)
        wl_ref[:, own] = jnp.zeros((CHAIN, BLOCK), bf16)
        wh_ref[own, :] = high
        wl_ref[own, :] = low
        for i in range(1, 8):
            turned_high, turned_low = split2(row[:, i * BLOCK : (i + 1) * BLOCK].T)
            uh_ref[i * BLOCK : (i + 1) * BLOCK, own] = turned_high
            ul_ref[i * BLOCK : (i + 1) * BLOCK, own] = turned_low

    def panel_step(k, carry):
        own = block_rows(k)
        following = jnp.minimum(k + 1, 7)
        after = block_rows(following)
        tiles = factor_tiles([d_ref[8 * t : 8 * t + 8, :] for t in range(16)])

        finish_row(jnp.maximum(k - 1, 0))
        left = (uh_ref[own, :], ul_ref[own, :])
        t_ref[...] = x_ref[own, :] - dot3(left, (wh_ref[...], wl_ref[...]))
        for t in range(16):
            t_ref[8 * t : 8 * t + 8, own] = jnp.where(lane == sub + 8 * t, f32(1.0), f32(0.0))
        left = (uh_ref[after, :], ul_ref[after, :])
        block = x_ref[after, after] - dot3(left, (wh_ref[:, after], wl_ref[:, after]))

        rows = pl.ds(pl.multiple_of(k * ROW_STEP, ROW_STEP), ROW_STEP)
        value = kernel_rows(feat_ref[rows, :], slice(0, COLUMNS))
        high, low = split2(value[:, :CHAIN])
        sh_ref[rows, :] = high
        sl_ref[rows, :] = low
        s2_ref[rows, :] = value[:, CHAIN:]

        lower = jnp.concatenate([jnp.where(lane <= sub + 8 * t, tiles[t], f32(0.0)) for t in range(16)], 0)
        lower_ref[...] = lower
        upper = dot3(split2(lower), split2(t_ref[:, after]))
        d_ref[...] = block - dot3(split2(upper.T), split2(upper))
        return carry

    lax.fori_loop(0, 8, panel_step, 0)
    finish_row(7)

    def add_hessian(panel, start):
        wide = iota((BLOCK, BLOCK), 1)

        def per_row(b, carry):
            first_row = start + b * BLOCK
            r = panel * WINDOW + 8 + (start // BLOCK) + b
            pick = wide == r
            own_offset = jnp.sum(jnp.where(pick, offc_ref[...], 0), axis=1, keepdims=True)
            own_weight = jnp.sum(jnp.where(pick, cc_ref[...], f32(0.0)), axis=1, keepdims=True)
            own_weight = jnp.where(first_row < PANEL, own_weight, f32(0.0))
            rows = block_rows(jnp.where(start < 0, b + (ROWS_DEV + start) // BLOCK, b + start // BLOCK))

            def value_at(which):
                s = panel * WINDOW + 8 + which
                partner_weight = jnp.where(first_row >= 0, cr_ref[pl.ds(s, 1), :], f32(0.0))
                return hessian_block(
                    first_row, which * BLOCK, (own_offset, own_weight),
                    (offr_ref[pl.ds(s, 1), :], partner_weight), dg_ref[pl.ds(panel * 4 + which, 1), :],
                )

            @pl.when(panel == 2)
            def _():
                s2_ref[rows, :] += value_at(c)

            @pl.when(panel < 2)
            def _():
                for d in range(4):
                    cols = pl.ds(pl.multiple_of(panel * PANEL + d * BLOCK, BLOCK), BLOCK)
                    value = sh_ref[rows, cols].astype(f32) + sl_ref[rows, cols].astype(f32) + value_at(d)
                    high, low = split2(value)
                    sh_ref[rows, cols] = high
                    sl_ref[rows, cols] = low

            return carry

        lax.fori_loop(0, jnp.where(start < 0, 8, 12), per_row, 0)

    @pl.when(r_rank <= 2)
    def _():
        add_hessian(r_rank, 0)

    next_panel = jnp.where(r_rank == 31, 0, r_rank + 1)

    @pl.when(next_panel <= 2)
    def _():
        add_hessian(next_panel, -1024)

    for panel in range(2):
        rows = pl.ds(pl.multiple_of(panel * PANEL + c * BLOCK, BLOCK), BLOCK)
        value = wh_ref[rows, :CHAIN].astype(f32) + wl_ref[rows, :CHAIN].astype(f32)
        for n in range(8):
            high, low = split2(value[:, n * BLOCK : (n + 1) * BLOCK].T)
            mh_ref[n * BLOCK : (n + 1) * BLOCK, panel * BLOCK : (panel + 1) * BLOCK] = high
            ml_ref[n * BLOCK : (n + 1) * BLOCK, panel * BLOCK : (panel + 1) * BLOCK] = low
    turned = jnp.concatenate(
        [
            (wh_ref[rows, CHAIN:].astype(f32) + wl_ref[rows, CHAIN:].astype(f32)).T
            for rows in (slice(i * BLOCK, (i + 1) * BLOCK) for i in range(8))
        ],
        1,
    )
    value = dot3(split2(turned), (wh_ref[:, :CHAIN], wl_ref[:, :CHAIN]))
    for n in range(8):
        high, low = split2(-value[:, n * BLOCK : (n + 1) * BLOCK].T)
        mh_ref[n * BLOCK : (n + 1) * BLOCK, 2 * BLOCK :] = high
        ml_ref[n * BLOCK : (n + 1) * BLOCK, 2 * BLOCK :] = low

    def copies(n):
        rows = pl.ds(pl.multiple_of(n * ROW_STEP, ROW_STEP), ROW_STEP)
        return [
            pltpu.make_async_copy(out_ref.at[0, rows], factor_hbm.at[0, rows], out_sem.at[n, 0]),
            pltpu.make_async_copy(out_ref.at[1, rows], factor_hbm.at[1, rows], out_sem.at[n, 1]),
            pltpu.make_async_copy(out_ref.at[2, rows], schur_hbm.at[rows], out_sem.at[n, 2]),
        ]

    def out_step(n, carry):
        rows = pl.ds(pl.multiple_of(n * ROW_STEP, ROW_STEP), ROW_STEP)
        both = (sh_ref[rows, :], sl_ref[rows, :])
        rest = dot3(both, (mh_ref[:, BLOCK:], ml_ref[:, BLOCK:]))
        both = (sh_ref[rows, :PANEL], sl_ref[rows, :PANEL])
        head = dot3(both, (mh_ref[:PANEL, :BLOCK], ml_ref[:PANEL, :BLOCK]))
        keep_second = jnp.where((r_rank == 0) & (n == 0), f32(0.0), f32(1.0))
        keep_schur = jnp.where((r_rank <= 1) & (n == 0), f32(0.0), f32(1.0))
        out_ref[0, rows, :] = head
        out_ref[1, rows, :] = rest[:, :BLOCK] * keep_second
        out_ref[2, rows, :] = (s2_ref[rows, :] + rest[:, BLOCK:]) * keep_schur
        for copy in copies(n):
            copy.start()
        return carry

    lax.fori_loop(0, ROW_STEPS, out_step, 0)
    for n in range(ROW_STEPS):
        for copy in copies(n):
            copy.wait()


def panel_chain(rank, mine, other, inv_length, features):
    vmem = pl.BlockSpec(memory_space=pltpu.VMEM)
    anywhere = pl.BlockSpec(memory_space=pl.ANY)
    return pl.pallas_call(
        chain_kernel,
        name="panel_chain",
        in_specs=[pl.BlockSpec(memory_space=pltpu.SMEM)] + [vmem] * 4,
        out_specs=(anywhere, anywhere),
        out_shape=(
            jax.ShapeDtypeStruct((2, ROWS_DEV, BLOCK), f32),
            jax.ShapeDtypeStruct((ROWS_DEV, BLOCK), f32),
        ),
        scratch_shapes=[
            pltpu.VMEM((CHAIN, COLUMNS), f32),
            pltpu.VMEM((16, BLOCK), f32),
            pltpu.VMEM((BLOCK, BLOCK), i32),
            pltpu.VMEM((BLOCK, BLOCK), f32),
            pltpu.VMEM((40, BLOCK), i32),
            pltpu.VMEM((40, BLOCK), f32),
            pltpu.VMEM((PANEL, COLUMNS), bf16),
            pltpu.VMEM((8, COLUMNS), f32),
            pltpu.VMEM((COLUMNS, BLOCK), f32),
            pltpu.VMEM((BLOCK, COLUMNS), f32),
            pltpu.VMEM((BLOCK, BLOCK), f32),
            pltpu.VMEM((BLOCK, BLOCK), f32),
            pltpu.VMEM((CHAIN, COLUMNS), bf16),
            pltpu.VMEM((CHAIN, COLUMNS), bf16),
            pltpu.VMEM((CHAIN, CHAIN), bf16),
            pltpu.VMEM((CHAIN, CHAIN), bf16),
            pltpu.VMEM((ROWS_DEV, CHAIN), bf16),
            pltpu.VMEM((ROWS_DEV, CHAIN), bf16),
            pltpu.VMEM((ROWS_DEV, BLOCK), f32),
            pltpu.VMEM((CHAIN, 3 * BLOCK), bf16),
            pltpu.VMEM((CHAIN, 3 * BLOCK), bf16),
            pltpu.VMEM((3, ROWS_DEV, BLOCK), f32),
            pltpu.SemaphoreType.DMA((ROW_STEPS, 3)),
        ],
        compiler_params=pltpu.CompilerParams(vmem_limit_bytes=VMEM_BYTES),
        cost_estimate=pl.CostEstimate(
            flops=6 * ROWS_DEV * COLUMNS * CHAIN, bytes_accessed=12 * 1024 * 1024, transcendentals=ROWS_DEV * COLUMNS
        ),
    )(rank, mine, other, inv_length, features)


def row_index(z, y, core):
    return (z % 4) * 8 + (y % 4) * 2 + core


def share_panels(features, nugget, tables):
    row = lax.axis_index("row")
    col = lax.axis_index("col")
    z, y = row // 8, (row // 2) % 4
    quarter = lax.dynamic_slice_in_dim(features, col * BLOCK, BLOCK, 0)
    extra = lax.dynamic_slice_in_dim(nugget, col * BLOCK, BLOCK, 0)[None, :]
    mine = jnp.concatenate([quarter, jnp.broadcast_to(extra, (8, BLOCK))], 0)

    def send(value, pairs):
        return lax.ppermute(value, "row", pairs)

    along_z = [
        send(mine, [(row_index(0, *at), row_index(k, *at)) for at in ((0, 0), (0, 1), (1, 0))]) for k in (1, 2, 3)
    ]
    for k in (1, 2, 3):
        mine = jnp.where(z == k, along_z[k - 1], mine)
    along_y = [
        send(
            mine,
            [
                (row_index(k, at, half), row_index(k, at + s, half))
                for k in range(4)
                for at, half in ((0, 0), (0, 1), (1, 0))
            ],
        )
        for s in (1, 2, 3)
    ]
    first, third = mine, mine
    for s in (1, 2, 3):
        first = jnp.where(y == s, along_y[s - 1], first)
        third = jnp.where(y == (1 + s) % 4, along_y[s - 1], third)
    part = jnp.concatenate([first, tables], 0)
    parts = [part] + [lax.ppermute(part, "col", [((i + k) % 4, i) for i in range(4)]) for k in (1, 2, 3)]
    summed = (parts[0][QUARTER:] + parts[1][QUARTER:]) + (parts[2][QUARTER:] + parts[3][QUARTER:])
    held = jnp.concatenate([part[:QUARTER] for part in parts] + [summed, third], 0)
    return held, send(held, [(i, i ^ 1) for i in range(32)])


def per_device(features, inv_length, nugget, pairs, weights):
    rank = jnp.stack([lax.axis_index("row"), lax.axis_index("col")]).astype(i32)
    tables = pair_tables(rank, pairs, weights.reshape(1, CONFIGS))
    mine, other = share_panels(features, nugget, tables)
    return panel_chain(rank, mine, other, inv_length.reshape(1, BLOCK), features)


def solution(mesh):
    placed = (P("row", None), P(), P("row"), P(), P())
    return jax.shard_map(
        per_device,
        mesh=mesh,
        in_specs=placed,
        out_specs=(P(None, "row", "col"), P("row", "col")),
        check_vma=False,
    )
```

time: 181 us -> 111 us (0.61)
  Pallas kernels: 148 us -> 75.2 us
  waiting for transfers between devices: 3.63 us -> 6.45 us
  starting transfers between devices: 24.4 us -> 22.3 us
    pallas_call x2 -> x1, Pallas kernels: 67.4 us -> 7.22 us  [pair_tables(): pl.pallas_call(tables_kernel, name='pair_tables', in_specs=[pl.BlockSpec(...]
    pallas_call x1, Pallas kernels: 80.5 us -> 68 us  [panel_chain(): pl.pallas_call(chain_kernel, name='panel_chain', in_specs=[pl.BlockSpec(m...]
    ppermute x3, waiting for transfers between devices: 0.01 us -> 4.42 us  [share_panels(): lax.ppermute(part, 'col', [((i + k) % 4, i) for i in range(4)])]
  transfers between devices with their start and end apart: 10 -> 10, of which waited for: 3 -> 5; matrix products, arithmetic and copies ran while one was open for 0% -> 1% of each run, Pallas kernels for 18% -> 7%
where the time goes in v2:
time: 111 us; the launch traced here: 110 us
  Pallas kernels  75.2 us (68%)
  starting transfers between devices  22.3 us (20%)
  waiting for transfers between devices  6.45 us (6%)
  other arithmetic  2.38 us (2%)
  local copies, waits for them, and re-layouts  2.37 us (2%)
    pallas_call x1, Pallas kernels, panel_chain(): pl.pallas_call(chain_kernel, name='panel_chain', in_specs=[pl.BlockSpec(m...  68 us
    ppermute x7, starting transfers between devices, send(): return lax.ppermute(value, 'row', pairs)  18 us
    pallas_call x1, Pallas kernels, pair_tables(): pl.pallas_call(tables_kernel, name='pair_tables', in_specs=[pl.BlockSpec(...  7.22 us
    ppermute x3, waiting for transfers between devices, share_panels(): lax.ppermute(part, 'col', [((i + k) % 4, i) for i in range(4)])  4.42 us
    ppermute x3, starting transfers between devices, share_panels(): lax.ppermute(part, 'col', [((i + k) % 4, i) for i in range(4)])  4.27 us
  transfers between devices with their start and end apart: 10, of which 5 were waited for; matrix products, arithmetic and copies ran while one was open for 1% of the time, Pallas kernels for 7%

profile of v2, /device:TPU:1, one launch (start us, length us, event | category | flops | bytes accessed | tf_op | source)
XLA Modules:
  0.0 109.6 jit_solution(7946422207696203614)
XLA Ops:
  0.6 0.8 dynamic_slice.7
  1.4 0.8 constant_dynamic-slice_fusion
  2.3 4.4 %collective-permute-start.2 = (f32[136,128]{1,0:T(8,128)S(1)}, f32[136,128]{1,0:T(8,128)S(1)}, u32[]{:S(2)}, u32[]{:S(2)}) collective-permute-start(f32[136,128]{1,0:T(8,128)S(1)} %pad_maximum_fusion.1), channel_id=1, source_target_pairs={{0,32},{4,36},{8,40},{1,33},{5,37},{9,41},{2,34},{6,38},{10,42},{3... | collective-permute-start | bytes 208904 | tf_op jit(solution)/shard_map/ppermute | solution.py:467
  6.6 2.6 %collective-permute-start.1 = (f32[136,128]{1,0:T(8,128)S(1)}, f32[136,128]{1,0:T(8,128)S(1)}, u32[]{:S(2)}, u32[]{:S(2)}) collective-permute-start(f32[136,128]{1,0:T(8,128)S(1)} %pad_maximum_fusion.1), channel_id=1, source_target_pairs={{0,64},{4,68},{8,72},{1,65},{5,69},{9,73},{2,66},{6,70},{10,74},{3... | collective-permute-start | bytes 208904 | tf_op jit(solution)/shard_map/ppermute | solution.py:467
  9.3 1.3 %collective-permute-start = (f32[136,128]{1,0:T(8,128)S(1)}, f32[136,128]{1,0:T(8,128)S(1)}, u32[]{:S(2)}, u32[]{:S(2)}) collective-permute-start(f32[136,128]{1,0:T(8,128)S(1)} %pad_maximum_fusion.1), channel_id=1, source_target_pairs={{0,96},{4,100},{8,104},{1,97},{5,101},{9,105},{2,98},{6,102},{10,1... | collective-permute-start | bytes 208904 | tf_op jit(solution)/shard_map/ppermute | solution.py:467
  10.6 0.7 pad_add_fusion.rank_ref
  11.3 0.0 collective-permute-done.2
  11.3 0.0 collective-permute-done.1
  11.3 0.7 collective-permute-done
  11.9 1.3 %collective-permute-start.5 = (f32[136,128]{1,0:T(8,128)S(1)}, f32[136,128]{1,0:T(8,128)S(1)}, u32[]{:S(2)}, u32[]{:S(2)}) collective-permute-start(f32[136,128]{1,0:T(8,128)S(1)} %select_select_fusion.1), channel_id=1, source_target_pairs={{0,8},{4,12},{8,16},{32,40},{36,44},{40,48},{64,72},{68,76},{72,80... | collective-permute-start | bytes 208904 | tf_op jit(solution)/shard_map/ppermute | solution.py:467
  13.2 1.3 %collective-permute-start.4 = (f32[136,128]{1,0:T(8,128)S(1)}, f32[136,128]{1,0:T(8,128)S(1)}, u32[]{:S(2)}, u32[]{:S(2)}) collective-permute-start(f32[136,128]{1,0:T(8,128)S(1)} %select_select_fusion.1), channel_id=1, source_target_pairs={{0,16},{4,20},{8,24},{32,48},{36,52},{40,56},{64,80},{68,84},{72,8... | collective-permute-start | bytes 208904 | tf_op jit(solution)/shard_map/ppermute | solution.py:467
  14.5 1.3 %collective-permute-start.3 = (f32[136,128]{1,0:T(8,128)S(1)}, f32[136,128]{1,0:T(8,128)S(1)}, u32[]{:S(2)}, u32[]{:S(2)}) collective-permute-start(f32[136,128]{1,0:T(8,128)S(1)} %select_select_fusion.1), channel_id=1, source_target_pairs={{0,24},{4,28},{8,0},{32,56},{36,60},{40,32},{64,88},{68,92},{72,64... | collective-permute-start | bytes 208904 | tf_op jit(solution)/shard_map/ppermute | solution.py:467
  15.8 7.2 %pair_tables.1 = f32[96,128]{1,0:T(8,128)} custom-call(s32[2]{0:T(128)} %pad_add_fusion.rank_ref, s32[2,131072]{1,0:T(2,128)} %pairs_ref.1, f32[1,131072]{1,0:T(1,128)} %bitcast.4), custom_call_target="tpu_custom_call" | custom-call | flops 8589934592 | bytes 1572864 | tf_op jit(solution)/shard_map/pair_tables/pallas_call | solution.py:112
  23.1 0.0 collective-permute-done.5
  23.1 0.0 collective-permute-done.4
  23.1 0.0 collective-permute-done.3
  23.1 0.8 pad_maximum_fusion
  23.9 2.5 %collective-permute-start.6 = (f32[232,128]{1,0:T(8,128)S(1)}, f32[232,128]{1,0:T(8,128)S(1)}, u32[]{:S(2)}, u32[]{:S(2)}) collective-permute-start(f32[232,128]{1,0:T(8,128)S(1)} %pad_maximum_fusion), channel_id=1, source_target_pairs={{1,0},{2,1},{3,2},{0,3},{5,4},{6,5},{7,6},{4,7},{9,8},{10,9},{11,1... | collective-permute-start | bytes 356360 | tf_op jit(solution)/shard_map/ppermute | solution.py:490
  26.5 0.0 collective-permute-start.8
  26.5 1.7 %collective-permute-start.7 = (f32[232,128]{1,0:T(8,128)S(1)}, f32[232,128]{1,0:T(8,128)S(1)}, u32[]{:S(2)}, u32[]{:S(2)}) collective-permute-start(f32[232,128]{1,0:T(8,128)S(1)} %pad_maximum_fusion), channel_id=1, source_target_pairs={{2,0},{3,1},{0,2},{1,3},{6,4},{7,5},{4,6},{5,7},{10,8},{11,9},{8,1... | collective-permute-start | bytes 356360 | tf_op jit(solution)/shard_map/ppermute | solution.py:490
  28.2 0.1 collective-permute-done.6
  28.3 3.5 %collective-permute-done.7 = f32[232,128]{1,0:T(8,128)S(1)} collective-permute-done((f32[232,128]{1,0:T(8,128)S(1)}, f32[232,128]{1,0:T(8,128)S(1)}, u32[]{:S(2)}, u32[]{:S(2)}) %collective-permute-start.7) | collective-permute-done | bytes 118816 | tf_op jit(solution)/shard_map/ppermute | solution.py:490
  31.8 0.8 collective-permute-done.8
  32.6 0.8 fusion.1
  33.5 0.0 copy-start
  33.5 5.9 %collective-permute-start.9 = (f32[776,128]{1,0:T(8,128)S(1)}, f32[776,128]{1,0:T(8,128)S(1)}, u32[]{:S(2)}, u32[]{:S(2)}) collective-permute-start(f32[776,128]{1,0:T(8,128)S(1)} %select_dynamic-update-slice_fusion.mine_ref), channel_id=1, source_target_pairs={{0,4},{4,0},{8,12},{12,8},{16,20},{20,16},{24,28},{28,24},{32,36},... | collective-permute-start | bytes 1191944 | tf_op jit(solution)/shard_map/ppermute | solution.py:467
  39.3 1.4 %collective-permute-done.9.other_ref = f32[776,128]{1,0:T(8,128)S(1)} collective-permute-done((f32[776,128]{1,0:T(8,128)S(1)}, f32[776,128]{1,0:T(8,128)S(1)}, u32[]{:S(2)}, u32[]{:S(2)}) %collective-permute-start.9) | collective-permute-done | bytes 397344 | tf_op jit(solution)/shard_map/ppermute | solution.py:467
  40.7 0.0 copy-start.1
  40.7 0.0 copy-done
  40.7 0.7 copy-done.1
  41.4 68.0 %panel_chain.1 = (f32[2,4096,128]{2,1,0:T(8,128)}, f32[4096,128]{1,0:T(8,128)}) custom-call(s32[2]{0:T(128)} %pad_add_fusion.rank_ref, f32[776,128]{1,0:T(8,128)} %copy-done, f32[776,128]{1,0:T(8,128)} %copy-done.1, f32[1,128]{1,0:T(1,128)} %bitcast.5, f32[4096,128]{1,0:T(8,128)} %feat_ref.1), custom_call_target="tpu_custom_call" | custom-call | flops 28991029248 | bytes 12582912 | tf_op jit(solution)/shard_map/panel_chain/pallas_call | solution.py:413
  (8 shorter events, 0.1 us)
Async XLA Ops:
  2.3 9.0 %collective-permute-start.2 = (f32[136,128]{1,0:T(8,128)S(1)}, f32[136,128]{1,0:T(8,128)S(1)}, u32[]{:S(2)}, u32[]{:S(2)}) collective-permute-start(f32[136,128]{1,0:T(8,128)S(1)} %pad_maximum_fusion.1), channel_id=1, source_target_pairs={{0,32},{4,36},{8,40},{1,33},{5,37},{9,41},{2,34},{6,38},{10,42},{3... | collective-permute-start | bytes 208904 | tf_op jit(solution)/shard_map/ppermute | solution.py:467
  6.6 4.6 %collective-permute-start.1 = (f32[136,128]{1,0:T(8,128)S(1)}, f32[136,128]{1,0:T(8,128)S(1)}, u32[]{:S(2)}, u32[]{:S(2)}) collective-permute-start(f32[136,128]{1,0:T(8,128)S(1)} %pad_maximum_fusion.1), channel_id=1, source_target_pairs={{0,64},{4,68},{8,72},{1,65},{5,69},{9,73},{2,66},{6,70},{10,74},{3... | collective-permute-start | bytes 208904 | tf_op jit(solution)/shard_map/ppermute | solution.py:467
  9.3 2.7 %collective-permute-start = (f32[136,128]{1,0:T(8,128)S(1)}, f32[136,128]{1,0:T(8,128)S(1)}, u32[]{:S(2)}, u32[]{:S(2)}) collective-permute-start(f32[136,128]{1,0:T(8,128)S(1)} %pad_maximum_fusion.1), channel_id=1, source_target_pairs={{0,96},{4,100},{8,104},{1,97},{5,101},{9,105},{2,98},{6,102},{10,1... | collective-permute-start | bytes 208904 | tf_op jit(solution)/shard_map/ppermute | solution.py:467
  11.9 11.1 %collective-permute-start.5 = (f32[136,128]{1,0:T(8,128)S(1)}, f32[136,128]{1,0:T(8,128)S(1)}, u32[]{:S(2)}, u32[]{:S(2)}) collective-permute-start(f32[136,128]{1,0:T(8,128)S(1)} %select_select_fusion.1), channel_id=1, source_target_pairs={{0,8},{4,12},{8,16},{32,40},{36,44},{40,48},{64,72},{68,76},{72,80... | collective-permute-start | bytes 208904 | tf_op jit(solution)/shard_map/ppermute | solution.py:467
  13.2 9.8 %collective-permute-start.4 = (f32[136,128]{1,0:T(8,128)S(1)}, f32[136,128]{1,0:T(8,128)S(1)}, u32[]{:S(2)}, u32[]{:S(2)}) collective-permute-start(f32[136,128]{1,0:T(8,128)S(1)} %select_select_fusion.1), channel_id=1, source_target_pairs={{0,16},{4,20},{8,24},{32,48},{36,52},{40,56},{64,80},{68,84},{72,8... | collective-permute-start | bytes 208904 | tf_op jit(solution)/shard_map/ppermute | solution.py:467
  14.5 8.5 %collective-permute-start.3 = (f32[136,128]{1,0:T(8,128)S(1)}, f32[136,128]{1,0:T(8,128)S(1)}, u32[]{:S(2)}, u32[]{:S(2)}) collective-permute-start(f32[136,128]{1,0:T(8,128)S(1)} %select_select_fusion.1), channel_id=1, source_target_pairs={{0,24},{4,28},{8,0},{32,56},{36,60},{40,32},{64,88},{68,92},{72,64... | collective-permute-start | bytes 208904 | tf_op jit(solution)/shard_map/ppermute | solution.py:467
  23.9 4.4 %collective-permute-start.6 = (f32[232,128]{1,0:T(8,128)S(1)}, f32[232,128]{1,0:T(8,128)S(1)}, u32[]{:S(2)}, u32[]{:S(2)}) collective-permute-start(f32[232,128]{1,0:T(8,128)S(1)} %pad_maximum_fusion), channel_id=1, source_target_pairs={{1,0},{2,1},{3,2},{0,3},{5,4},{6,5},{7,6},{4,7},{9,8},{10,9},{11,1... | collective-permute-start | bytes 356360 | tf_op jit(solution)/shard_map/ppermute | solution.py:490
  26.5 6.2 %collective-permute-start.8 = (f32[232,128]{1,0:T(8,128)S(1)}, f32[232,128]{1,0:T(8,128)S(1)}, u32[]{:S(2)}, u32[]{:S(2)}) collective-permute-start(f32[232,128]{1,0:T(8,128)S(1)} %pad_maximum_fusion), channel_id=1, source_target_pairs={{3,0},{0,1},{1,2},{2,3},{7,4},{4,5},{5,6},{6,7},{11,8},{8,9},{9,10... | collective-permute-start | bytes 356360 | tf_op jit(solution)/shard_map/ppermute | solution.py:490
  26.5 5.3 %collective-permute-start.7 = (f32[232,128]{1,0:T(8,128)S(1)}, f32[232,128]{1,0:T(8,128)S(1)}, u32[]{:S(2)}, u32[]{:S(2)}) collective-permute-start(f32[232,128]{1,0:T(8,128)S(1)} %pad_maximum_fusion), channel_id=1, source_target_pairs={{2,0},{3,1},{0,2},{1,3},{6,4},{7,5},{4,6},{5,7},{10,8},{11,9},{8,1... | collective-permute-start | bytes 356360 | tf_op jit(solution)/shard_map/ppermute | solution.py:490
  33.5 7.2 %copy-start = (f32[776,128]{1,0:T(8,128)}, f32[776,128]{1,0:T(8,128)S(1)}, u32[]{:S(2)}) copy-start(f32[776,128]{1,0:T(8,128)S(1)} %select_dynamic-update-slice_fusion.mine_ref) | copy-start | bytes 1191940
  33.5 7.2 %collective-permute-start.9 = (f32[776,128]{1,0:T(8,128)S(1)}, f32[776,128]{1,0:T(8,128)S(1)}, u32[]{:S(2)}, u32[]{:S(2)}) collective-permute-start(f32[776,128]{1,0:T(8,128)S(1)} %select_dynamic-update-slice_fusion.mine_ref), channel_id=1, source_target_pairs={{0,4},{4,0},{8,12},{12,8},{16,20},{20,16},{24,28},{28,24},{32,36},... | collective-permute-start | bytes 1191944 | tf_op jit(solution)/shard_map/ppermute | solution.py:467
  40.7 0.7 copy-start.1

commit v3 on v2

--- a/solution.py
+++ b/solution.py
@@ -1,3 +1,5 @@
+import functools
+
 import jax
 import jax.numpy as jnp
 from jax import lax
@@ -132,49 +134,76 @@
     return value + jnp.where(row == col, diagonal, f32(0.0))
 
 
-def factor_tiles(tiles):
+def lane_column(tile, at):
+    return jnp.broadcast_to(tile[:, at : at + 1], (8, BLOCK))
+
+
+def sublane_row(tile, at):
+    return jnp.broadcast_to(tile[at : at + 1, :], (8, BLOCK))
+
+
+HALF = 8
+
+
+def factor_tiles(tiles, beside):
     tiles = list(tiles)
     count = len(tiles)
     sub = iota((8, BLOCK), 0)
     lane = iota((8, BLOCK), 1)
-    for k in range(count):
-        base = 8 * k
-        inside = (lane >= base) & (lane < base + 8)
-        eye = jnp.where(lane == sub + base, f32(1.0), f32(0.0))
-        cols = [jnp.broadcast_to(tiles[k][:, base + j : base + j + 1], (8, BLOCK)) for j in range(8)]
-        entry = {}
-        for j in range(8):
-            for i in range(j, 8):
-                entry[i, j] = jnp.broadcast_to(cols[j][i : i + 1, :], (8, BLOCK))
-        own = jnp.where(inside, eye, tiles[k])
-        inverse = []
-        for j in range(8):
-            scale = 1.0 / entry[j, j]
-            inverse.append(scale)
-            ratio = {i: entry[i, j] * scale for i in range(j + 1, 8)}
-            for i in range(j + 1, 8):
-                for m in range(j + 1, i + 1):
-                    entry[i, m] = entry[i, m] - ratio[i] * entry[m, j]
-            if j < 7:
-                step = jnp.where(sub > j, cols[j] * scale, f32(0.0))
-                for m in range(j + 1, 8):
-                    cols[m] = cols[m] - step * entry[m, j]
-                own = own - step * jnp.broadcast_to(own[j : j + 1, :], (8, BLOCK))
-        rows = [jnp.broadcast_to(own[j : j + 1, :], (8, BLOCK)) for j in range(8)]
-        for t in range(k + 1, count):
-            tile = tiles[t]
-            left = [jnp.broadcast_to(tile[:, base + j : base + j + 1], (8, BLOCK)) for j in range(8)]
-            tile = jnp.where(inside, f32(0.0), tile)
+    for begin in range(0, count, HALF):
+        end = begin + HALF
+        cols = [lane_column(tiles[begin], 8 * begin + j) for j in range(8)]
+        for k in range(begin, end):
+            base = 8 * k
+            inside = (lane >= base) & (lane < base + 8)
+            eye = jnp.where(lane == sub + base, f32(1.0), f32(0.0))
+            entry = {(i, j): sublane_row(cols[j], i) for j in range(8) for i in range(j, 8)}
+            own = jnp.where(inside, eye, tiles[k])
+            if k < len(beside):
+                beside[k]()
+            rest = range(k + 1, end)
+            left = {t: [lane_column(tiles[t], base + j) for j in range(8)] for t in rest}
+            if k + 1 < end:
+                ahead = [lane_column(tiles[k + 1], base + 8 + m) for m in range(8)]
+            new = {t: jnp.where(inside, f32(0.0), tiles[t]) for t in rest}
+            inverse = []
             for j in range(8):
-                step = left[j] * inverse[j]
-                for m in range(j + 1, 8):
-                    left[m] = left[m] - step * entry[m, j]
-                tile = tile - step * rows[j]
-            tiles[t] = tile
-        scale = inverse[0]
-        for j in range(1, 8):
-            scale = jnp.where(sub == j, inverse[j], scale)
-        tiles[k] = own * jnp.sqrt(scale)
+                scale = 1.0 / entry[j, j]
+                inverse.append(scale)
+                ratio = {i: entry[i, j] * scale for i in range(j + 1, 8)}
+                for i in range(j + 1, 8):
+                    for m in range(j + 1, i + 1):
+                        entry[i, m] = entry[i, m] - ratio[i] * entry[m, j]
+                row = sublane_row(own, j)
+                if j < 7:
+                    step = jnp.where(sub > j, cols[j] * scale, f32(0.0))
+                    for m in range(j + 1, 8):
+                        cols[m] = cols[m] - step * entry[m, j]
+                    own = own - step * row
+                for t in rest:
+                    step = left[t][j] * scale
+                    if t == k + 1:
+                        for m in range(8):
+                            ahead[m] = ahead[m] - step * sublane_row(left[t][j], m)
+                    for m in range(j + 1, 8):
+                        left[t][m] = left[t][m] - step * entry[m, j]
+                    new[t] = new[t] - step * row
+            for t in rest:
+                tiles[t] = new[t]
+            scale = inverse[0]
+            for j in range(1, 8):
+                scale = jnp.where(sub == j, inverse[j], scale)
+            tiles[k] = own * jnp.sqrt(scale)
+            if k + 1 < end:
+                cols = ahead
+        if end < count:
+            rows = jnp.concatenate(tiles[begin:end], 0)
+            wide_lane, wide_sub = iota(rows.shape, 1), iota(rows.shape, 0) + 8 * begin
+            keep = (wide_lane <= wide_sub) | (wide_lane >= 8 * end)
+            product = dot3(split2(rows.T[8 * end :, :]), split2(jnp.where(keep, rows, f32(0.0))))
+            gone = (lane >= 8 * begin) & (lane < 8 * end)
+            for n, t in enumerate(range(end, count)):
+                tiles[t] = jnp.where(gone, f32(0.0), tiles[t]) - product[8 * n : 8 * n + 8, :]
     return tiles
 
 
@@ -268,95 +297,130 @@
     def block_rows(index):
         return pl.ds(pl.multiple_of(index * BLOCK, BLOCK), BLOCK)
 
-    def finish_row(k):
+    def finish_row(k, depth, turn_from):
         own = block_rows(k)
         row = dot3(split2(lower_ref[...]), split2(t_ref[...]))
         high, low = split2(row)
-        wh_ref[:, own] = jnp.zeros((CHAIN, BLOCK), bf16)
-        wl_ref[:, own] = jnp.zeros((CHAIN, BLOCK), bf16)
+        wh_ref[:depth, own] = jnp.zeros((depth, BLOCK), bf16)
+        wl_ref[:depth, own] = jnp.zeros((depth, BLOCK), bf16)
         wh_ref[own, :] = high
         wl_ref[own, :] = low
-        for i in range(1, 8):
+        for i in range(turn_from, 8):
             turned_high, turned_low = split2(row[:, i * BLOCK : (i + 1) * BLOCK].T)
             uh_ref[i * BLOCK : (i + 1) * BLOCK, own] = turned_high
             ul_ref[i * BLOCK : (i + 1) * BLOCK, own] = turned_low
 
-    def panel_step(k, carry):
+    def panel_step(k, depth, turn_from):
         own = block_rows(k)
         following = jnp.minimum(k + 1, 7)
         after = block_rows(following)
-        tiles = factor_tiles([d_ref[8 * t : 8 * t + 8, :] for t in range(16)])
-
-        finish_row(jnp.maximum(k - 1, 0))
-        left = (uh_ref[own, :], ul_ref[own, :])
-        t_ref[...] = x_ref[own, :] - dot3(left, (wh_ref[...], wl_ref[...]))
-        for t in range(16):
-            t_ref[8 * t : 8 * t + 8, own] = jnp.where(lane == sub + 8 * t, f32(1.0), f32(0.0))
-        left = (uh_ref[after, :], ul_ref[after, :])
-        block = x_ref[after, after] - dot3(left, (wh_ref[:, after], wl_ref[:, after]))
+        spans = [slice(n, min(n + 256, COLUMNS)) for n in range(0, COLUMNS, 256)]
 
         rows = pl.ds(pl.multiple_of(k * ROW_STEP, ROW_STEP), ROW_STEP)
-        value = kernel_rows(feat_ref[rows, :], slice(0, COLUMNS))
-        high, low = split2(value[:, :CHAIN])
-        sh_ref[rows, :] = high
-        sl_ref[rows, :] = low
-        s2_ref[rows, :] = value[:, CHAIN:]
+        high, middle, near = points_parts(feat_ref[rows, :], scale)
+        own_sq = -0.5 * jnp.sum(near * near, axis=1, keepdims=True)
+        parts = jnp.concatenate([high, high, middle, middle], 1)
+
+        def entries(cols):
+            value = jnp.exp2(dot_nn(parts, b4_ref[:, cols]) + (own_sq + csq_ref[0:1, cols]))
+            if cols.start == CHAIN:
+                s2_ref[rows, :] = value
+            else:
+                sh_ref[rows, cols], sl_ref[rows, cols] = split2(value)
+
+        finish_row(jnp.maximum(k - 1, 0), depth, turn_from)
+        left = (uh_ref[own, :depth], ul_ref[own, :depth])
+
+        def row_part(cols):
+            t_ref[:, cols] = x_ref[own, cols] - dot3(left, (wh_ref[:depth, cols], wl_ref[:depth, cols]))
+
+        def identity_part():
+            for t in range(16):
+                t_ref[8 * t : 8 * t + 8, own] = jnp.where(lane == sub + 8 * t, f32(1.0), f32(0.0))
+
+        block = []
+
+        def next_block():
+            other = (uh_ref[after, :depth], ul_ref[after, :depth])
+            block.append(x_ref[after, after] - dot3(other, (wh_ref[:depth, after], wl_ref[:depth, after])))
+
+        beside = [functools.partial(entries, cols) for cols in spans]
+        beside += [functools.partial(row_part, cols) for cols in spans] + [identity_part, next_block]
+        tiles = factor_tiles([d_ref[8 * t : 8 * t + 8, :] for t in range(16)], beside)
 
         lower = jnp.concatenate([jnp.where(lane <= sub + 8 * t, tiles[t], f32(0.0)) for t in range(16)], 0)
         lower_ref[...] = lower
         upper = dot3(split2(lower), split2(t_ref[:, after]))
-        d_ref[...] = block - dot3(split2(upper.T), split2(upper))
+        d_ref[...] = block[0] - dot3(split2(upper.T), split2(upper))
+
+    def first_half(k, carry):
+        panel_step(k, PANEL, 1)
         return carry
 
-    lax.fori_loop(0, 8, panel_step, 0)
-    finish_row(7)
-
-    def add_hessian(panel, start):
-        wide = iota((BLOCK, BLOCK), 1)
-
-        def per_row(b, carry):
-            first_row = start + b * BLOCK
-            r = panel * WINDOW + 8 + (start // BLOCK) + b
-            pick = wide == r
-            own_offset = jnp.sum(jnp.where(pick, offc_ref[...], 0), axis=1, keepdims=True)
-            own_weight = jnp.sum(jnp.where(pick, cc_ref[...], f32(0.0)), axis=1, keepdims=True)
-            own_weight = jnp.where(first_row < PANEL, own_weight, f32(0.0))
-            rows = block_rows(jnp.where(start < 0, b + (ROWS_DEV + start) // BLOCK, b + start // BLOCK))
-
-            def value_at(which):
-                s = panel * WINDOW + 8 + which
-                partner_weight = jnp.where(first_row >= 0, cr_ref[pl.ds(s, 1), :], f32(0.0))
-                return hessian_block(
-                    first_row, which * BLOCK, (own_offset, own_weight),
-                    (offr_ref[pl.ds(s, 1), :], partner_weight), dg_ref[pl.ds(panel * 4 + which, 1), :],
-                )
+    def second_half(k, carry):
+        panel_step(k, CHAIN, 4)
+        return carry
+
+    lax.fori_loop(0, 4, first_half, 0)
+    lax.fori_loop(4, 8, second_half, 0)
+    finish_row(7, CHAIN, 8)
+
+    def add_hessian(panel, first_row, device_row, count, from_row, from_col):
+        pick_lane = iota((BLOCK, BLOCK), 1)
+
+        def added(value, start, first_col, offset, weight, diagonal):
+            col = iota(value.shape, 1) + first_col
+            if from_row:
+                pick = pick_lane == panel * WINDOW + 8 + start // BLOCK
+                target = jnp.sum(jnp.where(pick, offc_ref[...], 0), axis=1, keepdims=True)
+                target = target + (iota((BLOCK, 1), 0) + start)
+                own_weight = jnp.sum(jnp.where(pick, cc_ref[...], f32(0.0)), axis=1, keepdims=True)
+                value = value - jnp.where(col == target, own_weight, f32(0.0))
+            if from_col:
+                row = iota(value.shape, 0) + start
+                target = iota((1, value.shape[1]), 1) + (first_col + offset)
+                value = value - jnp.where(row == target, weight, f32(0.0))
+                if from_row:
+                    value = value + jnp.where(row == col, diagonal, f32(0.0))
+            return value
+
+        def per_block(b, carry):
+            start = first_row + b * BLOCK
+            rows = block_rows(device_row // BLOCK + b)
 
             @pl.when(panel == 2)
             def _():
-                s2_ref[rows, :] += value_at(c)
+                at = pl.ds(2 * WINDOW + 8 + c, 1)
+                s2_ref[rows, :] = added(
+                    s2_ref[rows, :], start, c * BLOCK, offr_ref[at, :], cr_ref[at, :], dg_ref[pl.ds(8 + c, 1), :]
+                )
 
             @pl.when(panel < 2)
             def _():
-                for d in range(4):
-                    cols = pl.ds(pl.multiple_of(panel * PANEL + d * BLOCK, BLOCK), BLOCK)
-                    value = sh_ref[rows, cols].astype(f32) + sl_ref[rows, cols].astype(f32) + value_at(d)
-                    high, low = split2(value)
-                    sh_ref[rows, cols] = high
-                    sl_ref[rows, cols] = low
+                cols = pl.ds(pl.multiple_of(panel * PANEL, PANEL), PANEL)
+                lines = [panel * WINDOW + 8 + d for d in range(4)]
+                offset = jnp.concatenate([offr_ref[pl.ds(line, 1), :] for line in lines], 1)
+                weight = jnp.concatenate([cr_ref[pl.ds(line, 1), :] for line in lines], 1)
+                diagonal = jnp.concatenate([dg_ref[pl.ds(panel * 4 + d, 1), :] for d in range(4)], 1)
+                value = sh_ref[rows, cols].astype(f32) + sl_ref[rows, cols].astype(f32)
+                high, low = split2(added(value, start, 0, offset, weight, diagonal))
+                sh_ref[rows, cols] = high
+                sl_ref[rows, cols] = low
 
             return carry
 
-        lax.fori_loop(0, jnp.where(start < 0, 8, 12), per_row, 0)
+        lax.fori_loop(0, count, per_block, 0)
 
     @pl.when(r_rank <= 2)
     def _():
-        add_hessian(r_rank, 0)
+        add_hessian(r_rank, 0, 0, 4, True, True)
+        add_hessian(r_rank, PANEL, PANEL, 8, False, True)
 
     next_panel = jnp.where(r_rank == 31, 0, r_rank + 1)
 
     @pl.when(next_panel <= 2)
     def _():
-        add_hessian(next_panel, -1024)
+        add_hessian(next_panel, -1024, ROWS_DEV - 1024, 8, True, False)
 
     for panel in range(2):
         rows = pl.ds(pl.multiple_of(panel * PANEL + c * BLOCK, BLOCK), BLOCK)
@@ -391,7 +455,9 @@
         both = (sh_ref[rows, :], sl_ref[rows, :])
         rest = dot3(both, (mh_ref[:, BLOCK:], ml_ref[:, BLOCK:]))
         both = (sh_ref[rows, :PANEL], sl_ref[rows, :PANEL])
-        head = dot3(both, (mh_ref[:PANEL, :BLOCK], ml_ref[:PANEL, :BLOCK]))
+        packed = jnp.concatenate([mh_ref[:PANEL, :BLOCK], ml_ref[:PANEL, :BLOCK]], 1)
+        head = dot_nn(both[0], packed) + dot_nn(both[1], packed)
+        head = head[:, :BLOCK] + head[:, BLOCK:]
         keep_second = jnp.where((r_rank == 0) & (n == 0), f32(0.0), f32(1.0))
         keep_schur = jnp.where((r_rank <= 1) & (n == 0), f32(0.0), f32(1.0))
         out_ref[0, rows, :] = head

time: 111 us -> 95.4 us (0.86)
  Pallas kernels: 75.2 us -> 60.4 us
    pallas_call x1, Pallas kernels: 68 us -> 53.1 us  [panel_chain(): pl.pallas_call(chain_kernel, name='panel_chain', in_specs=[pl.BlockSpec(m...]
  transfers between devices with their start and end apart: 10 -> 10, of which waited for: 5 -> 5; matrix products, arithmetic and copies ran while one was open for 1% -> 1% of each run, Pallas kernels for 7% -> 8%
where the time goes in v3:
time: 95.4 us; the launch traced here: 94.9 us
  Pallas kernels  60.4 us (63%)
  starting transfers between devices  22.5 us (24%)
  waiting for transfers between devices  6.45 us (7%)
  other arithmetic  2.38 us (2%)
  local copies, waits for them, and re-layouts  2.37 us (2%)
    pallas_call x1, Pallas kernels, panel_chain(): pl.pallas_call(chain_kernel, name='panel_chain', in_specs=[pl.BlockSpec(m...  53.1 us
    ppermute x7, starting transfers between devices, send(): return lax.ppermute(value, 'row', pairs)  18.2 us
    pallas_call x1, Pallas kernels, pair_tables(): pl.pallas_call(tables_kernel, name='pair_tables', in_specs=[pl.BlockSpec(...  7.22 us
    ppermute x3, waiting for transfers between devices, share_panels(): lax.ppermute(part, 'col', [((i + k) % 4, i) for i in range(4)])  4.42 us
    ppermute x3, starting transfers between devices, share_panels(): lax.ppermute(part, 'col', [((i + k) % 4, i) for i in range(4)])  4.27 us
    ppermute x7, waiting for transfers between devices, send(): return lax.ppermute(value, 'row', pairs)  2.03 us
  transfers between devices with their start and end apart: 10, of which 5 were waited for; matrix products, arithmetic and copies ran while one was open for 1% of the time, Pallas kernels for 8%

profile of v3, /device:TPU:1, one launch (start us, length us, event | category | flops | bytes accessed | tf_op | source)
XLA Modules:
  0.0 94.9 jit_solution(18183139077485417760)
XLA Ops:
  0.6 0.8 dynamic_slice.7
  1.4 0.8 constant_dynamic-slice_fusion
  2.3 4.4 %collective-permute-start.2 = (f32[136,128]{1,0:T(8,128)S(1)}, f32[136,128]{1,0:T(8,128)S(1)}, u32[]{:S(2)}, u32[]{:S(2)}) collective-permute-start(f32[136,128]{1,0:T(8,128)S(1)} %pad_maximum_fusion.1), channel_id=1, source_target_pairs={{0,32},{4,36},{8,40},{1,33},{5,37},{9,41},{2,34},{6,38},{10,42},{3... | collective-permute-start | bytes 208904 | tf_op jit(solution)/shard_map/ppermute | solution.py:533
  6.6 2.6 %collective-permute-start.1 = (f32[136,128]{1,0:T(8,128)S(1)}, f32[136,128]{1,0:T(8,128)S(1)}, u32[]{:S(2)}, u32[]{:S(2)}) collective-permute-start(f32[136,128]{1,0:T(8,128)S(1)} %pad_maximum_fusion.1), channel_id=1, source_target_pairs={{0,64},{4,68},{8,72},{1,65},{5,69},{9,73},{2,66},{6,70},{10,74},{3... | collective-permute-start | bytes 208904 | tf_op jit(solution)/shard_map/ppermute | solution.py:533
  9.3 1.3 %collective-permute-start = (f32[136,128]{1,0:T(8,128)S(1)}, f32[136,128]{1,0:T(8,128)S(1)}, u32[]{:S(2)}, u32[]{:S(2)}) collective-permute-start(f32[136,128]{1,0:T(8,128)S(1)} %pad_maximum_fusion.1), channel_id=1, source_target_pairs={{0,96},{4,100},{8,104},{1,97},{5,101},{9,105},{2,98},{6,102},{10,1... | collective-permute-start | bytes 208904 | tf_op jit(solution)/shard_map/ppermute | solution.py:533
  10.6 0.7 pad_add_fusion.rank_ref
  11.3 0.0 collective-permute-done.2
  11.3 0.0 collective-permute-done.1
  11.3 0.7 collective-permute-done
  11.9 1.3 %collective-permute-start.5 = (f32[136,128]{1,0:T(8,128)S(1)}, f32[136,128]{1,0:T(8,128)S(1)}, u32[]{:S(2)}, u32[]{:S(2)}) collective-permute-start(f32[136,128]{1,0:T(8,128)S(1)} %select_select_fusion.1), channel_id=1, source_target_pairs={{0,8},{4,12},{8,16},{32,40},{36,44},{40,48},{64,72},{68,76},{72,80... | collective-permute-start | bytes 208904 | tf_op jit(solution)/shard_map/ppermute | solution.py:533
  13.2 1.3 %collective-permute-start.4 = (f32[136,128]{1,0:T(8,128)S(1)}, f32[136,128]{1,0:T(8,128)S(1)}, u32[]{:S(2)}, u32[]{:S(2)}) collective-permute-start(f32[136,128]{1,0:T(8,128)S(1)} %select_select_fusion.1), channel_id=1, source_target_pairs={{0,16},{4,20},{8,24},{32,48},{36,52},{40,56},{64,80},{68,84},{72,8... | collective-permute-start | bytes 208904 | tf_op jit(solution)/shard_map/ppermute | solution.py:533
  14.5 1.3 %collective-permute-start.3 = (f32[136,128]{1,0:T(8,128)S(1)}, f32[136,128]{1,0:T(8,128)S(1)}, u32[]{:S(2)}, u32[]{:S(2)}) collective-permute-start(f32[136,128]{1,0:T(8,128)S(1)} %select_select_fusion.1), channel_id=1, source_target_pairs={{0,24},{4,28},{8,0},{32,56},{36,60},{40,32},{64,88},{68,92},{72,64... | collective-permute-start | bytes 208904 | tf_op jit(solution)/shard_map/ppermute | solution.py:533
  15.8 7.2 %pair_tables.1 = f32[96,128]{1,0:T(8,128)} custom-call(s32[2]{0:T(128)} %pad_add_fusion.rank_ref, s32[2,131072]{1,0:T(2,128)} %pairs_ref.1, f32[1,131072]{1,0:T(1,128)} %bitcast.4), custom_call_target="tpu_custom_call" | custom-call | flops 8589934592 | bytes 1572864 | tf_op jit(solution)/shard_map/pair_tables/pallas_call | solution.py:114
  23.1 0.0 collective-permute-done.5
  23.1 0.0 collective-permute-done.4
  23.1 0.0 collective-permute-done.3
  23.1 0.8 pad_maximum_fusion
  23.9 2.5 %collective-permute-start.6 = (f32[232,128]{1,0:T(8,128)S(1)}, f32[232,128]{1,0:T(8,128)S(1)}, u32[]{:S(2)}, u32[]{:S(2)}) collective-permute-start(f32[232,128]{1,0:T(8,128)S(1)} %pad_maximum_fusion), channel_id=1, source_target_pairs={{1,0},{2,1},{3,2},{0,3},{5,4},{6,5},{7,6},{4,7},{9,8},{10,9},{11,1... | collective-permute-start | bytes 356360 | tf_op jit(solution)/shard_map/ppermute | solution.py:556
  26.5 0.0 collective-permute-start.8
  26.5 1.7 %collective-permute-start.7 = (f32[232,128]{1,0:T(8,128)S(1)}, f32[232,128]{1,0:T(8,128)S(1)}, u32[]{:S(2)}, u32[]{:S(2)}) collective-permute-start(f32[232,128]{1,0:T(8,128)S(1)} %pad_maximum_fusion), channel_id=1, source_target_pairs={{2,0},{3,1},{0,2},{1,3},{6,4},{7,5},{4,6},{5,7},{10,8},{11,9},{8,1... | collective-permute-start | bytes 356360 | tf_op jit(solution)/shard_map/ppermute | solution.py:556
  28.2 0.1 collective-permute-done.6
  28.3 3.5 %collective-permute-done.7 = f32[232,128]{1,0:T(8,128)S(1)} collective-permute-done((f32[232,128]{1,0:T(8,128)S(1)}, f32[232,128]{1,0:T(8,128)S(1)}, u32[]{:S(2)}, u32[]{:S(2)}) %collective-permute-start.7) | collective-permute-done | bytes 118816 | tf_op jit(solution)/shard_map/ppermute | solution.py:556
  31.8 0.8 collective-permute-done.8
  32.6 0.8 fusion.1
  33.5 0.0 copy-start
  33.5 6.0 %collective-permute-start.9 = (f32[776,128]{1,0:T(8,128)S(1)}, f32[776,128]{1,0:T(8,128)S(1)}, u32[]{:S(2)}, u32[]{:S(2)}) collective-permute-start(f32[776,128]{1,0:T(8,128)S(1)} %select_dynamic-update-slice_fusion.mine_ref), channel_id=1, source_target_pairs={{0,4},{4,0},{8,12},{12,8},{16,20},{20,16},{24,28},{28,24},{32,36},... | collective-permute-start | bytes 1191944 | tf_op jit(solution)/shard_map/ppermute | solution.py:533
  39.5 1.4 %collective-permute-done.9.other_ref = f32[776,128]{1,0:T(8,128)S(1)} collective-permute-done((f32[776,128]{1,0:T(8,128)S(1)}, f32[776,128]{1,0:T(8,128)S(1)}, u32[]{:S(2)}, u32[]{:S(2)}) %collective-permute-start.9) | collective-permute-done | bytes 397344 | tf_op jit(solution)/shard_map/ppermute | solution.py:533
  40.9 0.0 copy-start.1
  40.9 0.0 copy-done
  40.9 0.7 copy-done.1
  41.6 53.1 %panel_chain.1 = (f32[2,4096,128]{2,1,0:T(8,128)}, f32[4096,128]{1,0:T(8,128)}) custom-call(s32[2]{0:T(128)} %pad_add_fusion.rank_ref, f32[776,128]{1,0:T(8,128)} %copy-done, f32[776,128]{1,0:T(8,128)} %copy-done.1, f32[1,128]{1,0:T(1,128)} %bitcast.5, f32[4096,128]{1,0:T(8,128)} %feat_ref.1), custom_call_target="tpu_custom_call" | custom-call | flops 28991029248 | bytes 12582912 | tf_op jit(solution)/shard_map/panel_chain/pallas_call | solution.py:479
  (8 shorter events, 0.1 us)
Async XLA Ops:
  2.3 9.0 %collective-permute-start.2 = (f32[136,128]{1,0:T(8,128)S(1)}, f32[136,128]{1,0:T(8,128)S(1)}, u32[]{:S(2)}, u32[]{:S(2)}) collective-permute-start(f32[136,128]{1,0:T(8,128)S(1)} %pad_maximum_fusion.1), channel_id=1, source_target_pairs={{0,32},{4,36},{8,40},{1,33},{5,37},{9,41},{2,34},{6,38},{10,42},{3... | collective-permute-start | bytes 208904 | tf_op jit(solution)/shard_map/ppermute | solution.py:533
  6.6 4.6 %collective-permute-start.1 = (f32[136,128]{1,0:T(8,128)S(1)}, f32[136,128]{1,0:T(8,128)S(1)}, u32[]{:S(2)}, u32[]{:S(2)}) collective-permute-start(f32[136,128]{1,0:T(8,128)S(1)} %pad_maximum_fusion.1), channel_id=1, source_target_pairs={{0,64},{4,68},{8,72},{1,65},{5,69},{9,73},{2,66},{6,70},{10,74},{3... | collective-permute-start | bytes 208904 | tf_op jit(solution)/shard_map/ppermute | solution.py:533
  9.3 2.7 %collective-permute-start = (f32[136,128]{1,0:T(8,128)S(1)}, f32[136,128]{1,0:T(8,128)S(1)}, u32[]{:S(2)}, u32[]{:S(2)}) collective-permute-start(f32[136,128]{1,0:T(8,128)S(1)} %pad_maximum_fusion.1), channel_id=1, source_target_pairs={{0,96},{4,100},{8,104},{1,97},{5,101},{9,105},{2,98},{6,102},{10,1... | collective-permute-start | bytes 208904 | tf_op jit(solution)/shard_map/ppermute | solution.py:533
  11.9 11.1 %collective-permute-start.5 = (f32[136,128]{1,0:T(8,128)S(1)}, f32[136,128]{1,0:T(8,128)S(1)}, u32[]{:S(2)}, u32[]{:S(2)}) collective-permute-start(f32[136,128]{1,0:T(8,128)S(1)} %select_select_fusion.1), channel_id=1, source_target_pairs={{0,8},{4,12},{8,16},{32,40},{36,44},{40,48},{64,72},{68,76},{72,80... | collective-permute-start | bytes 208904 | tf_op jit(solution)/shard_map/ppermute | solution.py:533
  13.2 9.8 %collective-permute-start.4 = (f32[136,128]{1,0:T(8,128)S(1)}, f32[136,128]{1,0:T(8,128)S(1)}, u32[]{:S(2)}, u32[]{:S(2)}) collective-permute-start(f32[136,128]{1,0:T(8,128)S(1)} %select_select_fusion.1), channel_id=1, source_target_pairs={{0,16},{4,20},{8,24},{32,48},{36,52},{40,56},{64,80},{68,84},{72,8... | collective-permute-start | bytes 208904 | tf_op jit(solution)/shard_map/ppermute | solution.py:533
  14.5 8.5 %collective-permute-start.3 = (f32[136,128]{1,0:T(8,128)S(1)}, f32[136,128]{1,0:T(8,128)S(1)}, u32[]{:S(2)}, u32[]{:S(2)}) collective-permute-start(f32[136,128]{1,0:T(8,128)S(1)} %select_select_fusion.1), channel_id=1, source_target_pairs={{0,24},{4,28},{8,0},{32,56},{36,60},{40,32},{64,88},{68,92},{72,64... | collective-permute-start | bytes 208904 | tf_op jit(solution)/shard_map/ppermute | solution.py:533
  23.9 4.4 %collective-permute-start.6 = (f32[232,128]{1,0:T(8,128)S(1)}, f32[232,128]{1,0:T(8,128)S(1)}, u32[]{:S(2)}, u32[]{:S(2)}) collective-permute-start(f32[232,128]{1,0:T(8,128)S(1)} %pad_maximum_fusion), channel_id=1, source_target_pairs={{1,0},{2,1},{3,2},{0,3},{5,4},{6,5},{7,6},{4,7},{9,8},{10,9},{11,1... | collective-permute-start | bytes 356360 | tf_op jit(solution)/shard_map/ppermute | solution.py:556
  26.5 6.2 %collective-permute-start.8 = (f32[232,128]{1,0:T(8,128)S(1)}, f32[232,128]{1,0:T(8,128)S(1)}, u32[]{:S(2)}, u32[]{:S(2)}) collective-permute-start(f32[232,128]{1,0:T(8,128)S(1)} %pad_maximum_fusion), channel_id=1, source_target_pairs={{3,0},{0,1},{1,2},{2,3},{7,4},{4,5},{5,6},{6,7},{11,8},{8,9},{9,10... | collective-permute-start | bytes 356360 | tf_op jit(solution)/shard_map/ppermute | solution.py:556
  26.5 5.3 %collective-permute-start.7 = (f32[232,128]{1,0:T(8,128)S(1)}, f32[232,128]{1,0:T(8,128)S(1)}, u32[]{:S(2)}, u32[]{:S(2)}) collective-permute-start(f32[232,128]{1,0:T(8,128)S(1)} %pad_maximum_fusion), channel_id=1, source_target_pairs={{2,0},{3,1},{0,2},{1,3},{6,4},{7,5},{4,6},{5,7},{10,8},{11,9},{8,1... | collective-permute-start | bytes 356360 | tf_op jit(solution)/shard_map/ppermute | solution.py:556
  33.5 7.4 %copy-start = (f32[776,128]{1,0:T(8,128)}, f32[776,128]{1,0:T(8,128)S(1)}, u32[]{:S(2)}) copy-start(f32[776,128]{1,0:T(8,128)S(1)} %select_dynamic-update-slice_fusion.mine_ref) | copy-start | bytes 1191940
  33.5 7.4 %collective-permute-start.9 = (f32[776,128]{1,0:T(8,128)S(1)}, f32[776,128]{1,0:T(8,128)S(1)}, u32[]{:S(2)}, u32[]{:S(2)}) collective-permute-start(f32[776,128]{1,0:T(8,128)S(1)} %select_dynamic-update-slice_fusion.mine_ref), channel_id=1, source_target_pairs={{0,4},{4,0},{8,12},{12,8},{16,20},{20,16},{24,28},{28,24},{32,36},... | collective-permute-start | bytes 1191944 | tf_op jit(solution)/shard_map/ppermute | solution.py:533
  40.9 0.7 copy-start.1

commit v4 on v3

--- a/solution.py
+++ b/solution.py
@@ -17,7 +17,7 @@
 ROW_STEP = 512
 ROW_STEPS = ROWS_DEV // ROW_STEP
 ROOT_LOG2E = 1.2011224087864498
-VMEM_BYTES = 56 * 1024 * 1024
+VMEM_BYTES = 50 * 1024 * 1024
 HIGHEST = lax.Precision.HIGHEST
 f32, bf16, i32 = jnp.float32, jnp.bfloat16, jnp.int32
 
@@ -51,8 +51,9 @@
     return high, (value - high.astype(f32)).astype(bf16)
 
 
-TABLE_CHUNK = 2048
+TABLE_CHUNK = 4096
 TABLE_ROWS = 96
+TABLE_SHARE = CONFIGS // 8
 QUARTER = BLOCK + 8
 
 
@@ -62,11 +63,9 @@
     code = jnp.where(row < 36, code, -1)
     low_id = iota((BLOCK, 1), 0)
     acc_ref[...] = jnp.zeros_like(acc_ref)
-    share = CONFIGS // 8
-    start = (2 * rank_ref[1] + (rank_ref[0] & 1)) * share
 
     def step(index, carry):
-        span = pl.ds(pl.multiple_of(start + index * TABLE_CHUNK, TABLE_CHUNK), TABLE_CHUNK)
+        span = pl.ds(pl.multiple_of(index * TABLE_CHUNK, TABLE_CHUNK), TABLE_CHUNK)
         winner = pairs_ref[0:1, span]
         loser = pairs_ref[1:2, span]
         weight = weights_ref[0:1, span]
@@ -78,11 +77,11 @@
         parts += [part.astype(f32) for part in split3(weight)]
         values = [jnp.where(hit, part, f32(0.0)) for part in parts]
         values.append(jnp.zeros((8, TABLE_CHUNK), f32))
-        acc_ref[:, 0:208] += dot_nt(one_hot, jnp.concatenate(values, 0).astype(bf16))
+        acc_ref[...] += dot_nt(jnp.concatenate(values, 0).astype(bf16), one_hot)
         return carry
 
-    lax.fori_loop(0, share // TABLE_CHUNK, step, 0)
-    turned = acc_ref[...].T
+    lax.fori_loop(0, TABLE_SHARE // TABLE_CHUNK, step, 0)
+    turned = acc_ref[...]
     offr = turned[0:40] * 32.0 + turned[40:80]
     cr = turned[80:120] + turned[120:160] + turned[160:200]
     out_ref[0:40, :] = offr
@@ -99,7 +98,7 @@
             target = jnp.broadcast_to(offc[:, r : r + 1] + (place + BLOCK * (h - 8)), (BLOCK, BLOCK)) - lane
             weight = jnp.broadcast_to(cc[:, r : r + 1], (BLOCK, BLOCK))
             for d in range(4):
-                if h - 8 <= d:
+                if d <= h <= d + 8:
                     found = jnp.where(target == BLOCK * d, weight, f32(0.0))
                     lost[d] = lost[d] + jnp.sum(found, axis=0, keepdims=True)
         for d in range(4):
@@ -110,28 +109,25 @@
 
 
 def pair_tables(rank, pairs, weights):
-    vmem = pl.BlockSpec(memory_space=pltpu.VMEM)
+    def share(n, rank_ref):
+        return 0, 2 * rank_ref[1] + (rank_ref[0] & 1)
+
     return pl.pallas_call(
         tables_kernel,
         name="pair_tables",
-        in_specs=[pl.BlockSpec(memory_space=pltpu.SMEM), vmem, vmem],
+        grid_spec=pltpu.PrefetchScalarGridSpec(
+            num_scalar_prefetch=1,
+            grid=(1,),
+            in_specs=[pl.BlockSpec((2, TABLE_SHARE), share), pl.BlockSpec((1, TABLE_SHARE), share)],
+            out_specs=pl.BlockSpec((TABLE_ROWS, BLOCK), lambda n, rank_ref: (0, 0)),
+            scratch_shapes=[pltpu.VMEM((208, BLOCK), f32)],
+        ),
         out_shape=jax.ShapeDtypeStruct((TABLE_ROWS, BLOCK), f32),
-        scratch_shapes=[pltpu.VMEM((BLOCK, 256), f32)],
         compiler_params=pltpu.CompilerParams(vmem_limit_bytes=VMEM_BYTES),
         cost_estimate=pl.CostEstimate(
             flops=2 * CONFIGS * BLOCK * 256, bytes_accessed=12 * CONFIGS, transcendentals=0
         ),
     )(rank, pairs, weights)
-
-
-def hessian_block(first_row, first_col, own, partner, diagonal):
-    row = iota((BLOCK, BLOCK), 0) + first_row
-    col = iota((BLOCK, BLOCK), 1) + first_col
-    own_offset, own_weight = own
-    partner_offset, partner_weight = partner
-    value = jnp.where(row + own_offset == col, -own_weight, f32(0.0))
-    value = value + jnp.where(col + partner_offset == row, -partner_weight, f32(0.0))
-    return value + jnp.where(row == col, diagonal, f32(0.0))
 
 
 def lane_column(tile, at):
@@ -219,13 +215,15 @@
 
 
 def chain_kernel(
-    rank_ref, mine_ref, other_ref, inv_ref, feat_ref, factor_hbm, schur_hbm,
+    rank_ref, mine_ref, other_ref, inv_ref, feat_hbm, factor_hbm, schur_hbm,
     x_ref, dg_ref, offc_ref, cc_ref, offr_ref, cr_ref, b4_ref, csq_ref, pts_ref, t_ref, lower_ref, d_ref,
-    wh_ref, wl_ref, uh_ref, ul_ref, sh_ref, sl_ref, s2_ref, mh_ref, ml_ref, out_ref, out_sem,
+    wh_ref, wl_ref, uh_ref, ul_ref, sh_ref, sl_ref, s2_ref, mh_ref, ml_ref, out_ref, feat_ref, out_sem, feat_sem,
 ):
     r_rank = rank_ref[0]
     c = rank_ref[1]
     even = (r_rank & 1) == 0
+    feat_copy = pltpu.make_async_copy(feat_hbm, feat_ref, feat_sem)
+    feat_copy.start()
     scale = inv_ref[...] * ROOT_LOG2E
 
     def of_panel(panel, rows):
@@ -266,36 +264,51 @@
         inner = dot_nn(jnp.concatenate([high, high, middle, middle], 1), b4_ref[:, cols])
         return jnp.exp2(inner + (own_sq + csq_ref[0:1, cols]))
 
-    for k in range(8):
-        rows = slice(k * BLOCK, (k + 1) * BLOCK)
-        x_ref[rows, k * BLOCK :] = kernel_rows(pts_ref[rows, :], slice(k * BLOCK, COLUMNS))
-        if k:
-            x_ref[rows, : k * BLOCK] = jnp.zeros((BLOCK, k * BLOCK), f32)
     for ref in (wh_ref, wl_ref, uh_ref, ul_ref, t_ref, lower_ref):
         ref[...] = jnp.zeros_like(ref)
-    for panel in range(2):
-        for b in range(4):
-            r = panel * WINDOW + 8 + b
-            for d in range(b, 4):
-                s = panel * WINDOW + 8 + d
-                at = (
-                    slice(panel * PANEL + b * BLOCK, panel * PANEL + (b + 1) * BLOCK),
-                    slice(panel * PANEL + d * BLOCK, panel * PANEL + (d + 1) * BLOCK),
-                )
-                line = panel * 4 + d
-                x_ref[at] += hessian_block(
-                    b * BLOCK, d * BLOCK,
-                    (offc_ref[:, r : r + 1], cc_ref[:, r : r + 1]),
-                    (offr_ref[s : s + 1, :], cr_ref[s : s + 1, :]),
-                    dg_ref[line : line + 1, :],
-                )
-
     sub = iota((8, BLOCK), 0)
     lane = iota((8, BLOCK), 1)
-    d_ref[...] = x_ref[:BLOCK, :BLOCK]
 
     def block_rows(index):
         return pl.ds(pl.multiple_of(index * BLOCK, BLOCK), BLOCK)
+
+    def added(value, panel, start, first_col, lines, from_row, from_col):
+        offset, weight, diagonal = lines
+        col = iota(value.shape, 1) + first_col
+        if from_row:
+            pick = iota((BLOCK, BLOCK), 1) == panel * WINDOW + 8 + start // BLOCK
+            target = jnp.sum(jnp.where(pick, offc_ref[...], 0), axis=1, keepdims=True)
+            target = target + (iota((BLOCK, 1), 0) + start)
+            own_weight = jnp.sum(jnp.where(pick, cc_ref[...], f32(0.0)), axis=1, keepdims=True)
+            value = value - jnp.where(col == target, own_weight, f32(0.0))
+        if from_col:
+            row = iota(value.shape, 0) + start
+            target = iota((1, value.shape[1]), 1) + (first_col + offset)
+            value = value - jnp.where(row == target, weight, f32(0.0))
+            if from_row:
+                value = value + jnp.where(row == col, diagonal, f32(0.0))
+        return value
+
+    def panel_lines(panel):
+        at = [pl.ds(panel * WINDOW + 8 + d, 1) for d in range(4)]
+        return (
+            jnp.concatenate([offr_ref[line, :] for line in at], 1),
+            jnp.concatenate([cr_ref[line, :] for line in at], 1),
+            jnp.concatenate([dg_ref[pl.ds(panel * 4 + d, 1), :] for d in range(4)], 1),
+        )
+
+    def system_row(i):
+        rows = block_rows(i)
+        value = kernel_rows(pts_ref[rows, :], slice(0, COLUMNS))
+        x_ref[rows, :] = jnp.where(iota((BLOCK, COLUMNS), 1) >= i * BLOCK, value, f32(0.0))
+        panel, start = i // 4, (i % 4) * BLOCK
+        cols = pl.ds(pl.multiple_of(panel * PANEL, PANEL), PANEL)
+        value = added(x_ref[rows, cols], panel, start, 0, panel_lines(panel), True, True)
+        x_ref[rows, cols] = jnp.where(iota((BLOCK, PANEL), 1) >= start, value, f32(0.0))
+
+    for i in range(8):
+        system_row(i)
+    d_ref[...] = x_ref[:BLOCK, :BLOCK]
 
     def finish_row(k, depth, turn_from):
         own = block_rows(k)
@@ -361,29 +374,12 @@
         panel_step(k, CHAIN, 4)
         return carry
 
+    feat_copy.wait()
     lax.fori_loop(0, 4, first_half, 0)
     lax.fori_loop(4, 8, second_half, 0)
     finish_row(7, CHAIN, 8)
 
     def add_hessian(panel, first_row, device_row, count, from_row, from_col):
-        pick_lane = iota((BLOCK, BLOCK), 1)
-
-        def added(value, start, first_col, offset, weight, diagonal):
-            col = iota(value.shape, 1) + first_col
-            if from_row:
-                pick = pick_lane == panel * WINDOW + 8 + start // BLOCK
-                target = jnp.sum(jnp.where(pick, offc_ref[...], 0), axis=1, keepdims=True)
-                target = target + (iota((BLOCK, 1), 0) + start)
-                own_weight = jnp.sum(jnp.where(pick, cc_ref[...], f32(0.0)), axis=1, keepdims=True)
-                value = value - jnp.where(col == target, own_weight, f32(0.0))
-            if from_col:
-                row = iota(value.shape, 0) + start
-                target = iota((1, value.shape[1]), 1) + (first_col + offset)
-                value = value - jnp.where(row == target, weight, f32(0.0))
-                if from_row:
-                    value = value + jnp.where(row == col, diagonal, f32(0.0))
-            return value
-
         def per_block(b, carry):
             start = first_row + b * BLOCK
             rows = block_rows(device_row // BLOCK + b)
@@ -391,19 +387,14 @@
             @pl.when(panel == 2)
             def _():
                 at = pl.ds(2 * WINDOW + 8 + c, 1)
-                s2_ref[rows, :] = added(
-                    s2_ref[rows, :], start, c * BLOCK, offr_ref[at, :], cr_ref[at, :], dg_ref[pl.ds(8 + c, 1), :]
-                )
+                lines = (offr_ref[at, :], cr_ref[at, :], dg_ref[pl.ds(8 + c, 1), :])
+                s2_ref[rows, :] = added(s2_ref[rows, :], panel, start, c * BLOCK, lines, from_row, from_col)
 
             @pl.when(panel < 2)
             def _():
                 cols = pl.ds(pl.multiple_of(panel * PANEL, PANEL), PANEL)
-                lines = [panel * WINDOW + 8 + d for d in range(4)]
-                offset = jnp.concatenate([offr_ref[pl.ds(line, 1), :] for line in lines], 1)
-                weight = jnp.concatenate([cr_ref[pl.ds(line, 1), :] for line in lines], 1)
-                diagonal = jnp.concatenate([dg_ref[pl.ds(panel * 4 + d, 1), :] for d in range(4)], 1)
                 value = sh_ref[rows, cols].astype(f32) + sl_ref[rows, cols].astype(f32)
-                high, low = split2(added(value, start, 0, offset, weight, diagonal))
+                high, low = split2(added(value, panel, start, 0, panel_lines(panel), from_row, from_col))
                 sh_ref[rows, cols] = high
                 sl_ref[rows, cols] = low
 
@@ -479,7 +470,7 @@
     return pl.pallas_call(
         chain_kernel,
         name="panel_chain",
-        in_specs=[pl.BlockSpec(memory_space=pltpu.SMEM)] + [vmem] * 4,
+        in_specs=[pl.BlockSpec(memory_space=pltpu.SMEM)] + [vmem] * 3 + [anywhere],
         out_specs=(anywhere, anywhere),
         out_shape=(
             jax.ShapeDtypeStruct((2, ROWS_DEV, BLOCK), f32),
@@ -508,7 +499,9 @@
             pltpu.VMEM((CHAIN, 3 * BLOCK), bf16),
             pltpu.VMEM((CHAIN, 3 * BLOCK), bf16),
             pltpu.VMEM((3, ROWS_DEV, BLOCK), f32),
+            pltpu.VMEM((ROWS_DEV, BLOCK), f32),
             pltpu.SemaphoreType.DMA((ROW_STEPS, 3)),
+            pltpu.SemaphoreType.DMA,
         ],
         compiler_params=pltpu.CompilerParams(vmem_limit_bytes=VMEM_BYTES),
         cost_estimate=pl.CostEstimate(
@@ -526,7 +519,7 @@
     col = lax.axis_index("col")
     z, y = row // 8, (row // 2) % 4
     quarter = lax.dynamic_slice_in_dim(features, col * BLOCK, BLOCK, 0)
-    extra = lax.dynamic_slice_in_dim(nugget, col * BLOCK, BLOCK, 0)[None, :]
+    extra = lax.dynamic_slice_in_dim(nugget.reshape(ROWS_DEV // BLOCK, BLOCK), col, 1, 0)
     mine = jnp.concatenate([quarter, jnp.broadcast_to(extra, (8, BLOCK))], 0)
 
     def send(value, pairs):

time: 95.4 us -> 92 us (0.964)
  Pallas kernels: 60.4 us -> 57.1 us
  other arithmetic: 2.38 us -> 0.19 us
  local copies, waits for them, and re-layouts: 2.37 us -> 3.85 us
    pallas_call x1, Pallas kernels: 7.22 us -> 4.63 us  [pair_tables(): pl.pallas_call(tables_kernel, name='pair_tables', grid_spec=pltpu.Prefetc...]
    unnamed x7 -> x13, local copies, waits for them, and re-layouts: 0.76 us -> 3 us
  transfers between devices with their start and end apart: 10 -> 10, of which waited for: 5 -> 5; matrix products, arithmetic and copies ran while one was open for 1% -> 0% of each run, Pallas kernels for 8% -> 5%
where the time goes in v4:
time: 92 us; the launch traced here: 91.6 us
  Pallas kernels  57.1 us (62%)
  starting transfers between devices  22.5 us (24%)
  waiting for transfers between devices  7.03 us (8%)
  local copies, waits for them, and re-layouts  3.85 us (4%)
  between operations  0.97 us (1%)
    pallas_call x1, Pallas kernels, panel_chain(): pl.pallas_call(chain_kernel, name='panel_chain', in_specs=[pl.BlockSpec(m...  52.5 us
    ppermute x7, starting transfers between devices, send(): return lax.ppermute(value, 'row', pairs)  18.2 us
    pallas_call x1, Pallas kernels, pair_tables(): pl.pallas_call(tables_kernel, name='pair_tables', grid_spec=pltpu.Prefetc...  4.63 us
    ppermute x3, waiting for transfers between devices, share_panels(): lax.ppermute(part, 'col', [((i + k) % 4, i) for i in range(4)])  4.42 us
    ppermute x3, starting transfers between devices, share_panels(): lax.ppermute(part, 'col', [((i + k) % 4, i) for i in range(4)])  4.28 us
    unnamed x13, local copies, waits for them, and re-layouts  3 us
    ppermute x7, waiting for transfers between devices, send(): return lax.ppermute(value, 'row', pairs)  2.61 us
  transfers between devices with their start and end apart: 10, of which 5 were waited for; matrix products, arithmetic and copies ran while one was open for 0% of the time, Pallas kernels for 5%

profile of v4, /device:TPU:1, one launch (start us, length us, event | category | flops | bytes accessed | tf_op | source)
XLA Modules:
  0.0 91.6 jit_solution(17442396367139036312)
XLA Ops:
  0.6 0.0 copy-start
  0.6 0.7 copy-done
  1.4 0.8 constant_dynamic-slice_fusion
  2.2 4.4 %collective-permute-start.2 = (f32[136,128]{1,0:T(8,128)S(1)}, f32[136,128]{1,0:T(8,128)S(1)}, u32[]{:S(2)}, u32[]{:S(2)}) collective-permute-start(f32[136,128]{1,0:T(8,128)S(1)} %pad_maximum_fusion.1), channel_id=1, source_target_pairs={{0,32},{4,36},{8,40},{1,33},{5,37},{9,41},{2,34},{6,38},{10,42},{3... | collective-permute-start | bytes 208904 | tf_op jit(solution)/shard_map/ppermute | solution.py:526
  6.6 2.6 %collective-permute-start.1 = (f32[136,128]{1,0:T(8,128)S(1)}, f32[136,128]{1,0:T(8,128)S(1)}, u32[]{:S(2)}, u32[]{:S(2)}) collective-permute-start(f32[136,128]{1,0:T(8,128)S(1)} %pad_maximum_fusion.1), channel_id=1, source_target_pairs={{0,64},{4,68},{8,72},{1,65},{5,69},{9,73},{2,66},{6,70},{10,74},{3... | collective-permute-start | bytes 208904 | tf_op jit(solution)/shard_map/ppermute | solution.py:526
  9.2 1.3 %collective-permute-start = (f32[136,128]{1,0:T(8,128)S(1)}, f32[136,128]{1,0:T(8,128)S(1)}, u32[]{:S(2)}, u32[]{:S(2)}) collective-permute-start(f32[136,128]{1,0:T(8,128)S(1)} %pad_maximum_fusion.1), channel_id=1, source_target_pairs={{0,96},{4,100},{8,104},{1,97},{5,101},{9,105},{2,98},{6,102},{10,1... | collective-permute-start | bytes 208904 | tf_op jit(solution)/shard_map/ppermute | solution.py:526
  10.6 0.1 pad_add_fusion.rank_ref
  10.6 0.0 collective-permute-done.2
  10.6 0.0 collective-permute-done.1
  10.6 1.2 %collective-permute-done = f32[136,128]{1,0:T(8,128)S(1)} collective-permute-done((f32[136,128]{1,0:T(8,128)S(1)}, f32[136,128]{1,0:T(8,128)S(1)}, u32[]{:S(2)}, u32[]{:S(2)}) %collective-permute-start) | collective-permute-done | bytes 69664 | tf_op jit(solution)/shard_map/ppermute | solution.py:526
  11.9 1.3 %collective-permute-start.5 = (f32[136,128]{1,0:T(8,128)S(1)}, f32[136,128]{1,0:T(8,128)S(1)}, u32[]{:S(2)}, u32[]{:S(2)}) collective-permute-start(f32[136,128]{1,0:T(8,128)S(1)} %select_select_fusion.1), channel_id=1, source_target_pairs={{0,8},{4,12},{8,16},{32,40},{36,44},{40,48},{64,72},{68,76},{72,80... | collective-permute-start | bytes 208904 | tf_op jit(solution)/shard_map/ppermute | solution.py:526
  13.2 1.3 %collective-permute-start.4 = (f32[136,128]{1,0:T(8,128)S(1)}, f32[136,128]{1,0:T(8,128)S(1)}, u32[]{:S(2)}, u32[]{:S(2)}) collective-permute-start(f32[136,128]{1,0:T(8,128)S(1)} %select_select_fusion.1), channel_id=1, source_target_pairs={{0,16},{4,20},{8,24},{32,48},{36,52},{40,56},{64,80},{68,84},{72,8... | collective-permute-start | bytes 208904 | tf_op jit(solution)/shard_map/ppermute | solution.py:526
  14.5 1.3 %collective-permute-start.3 = (f32[136,128]{1,0:T(8,128)S(1)}, f32[136,128]{1,0:T(8,128)S(1)}, u32[]{:S(2)}, u32[]{:S(2)}) collective-permute-start(f32[136,128]{1,0:T(8,128)S(1)} %select_select_fusion.1), channel_id=1, source_target_pairs={{0,24},{4,28},{8,0},{32,56},{36,60},{40,32},{64,88},{68,92},{72,64... | collective-permute-start | bytes 208904 | tf_op jit(solution)/shard_map/ppermute | solution.py:526
  15.8 0.0 copy-start.2
  15.8 1.2 %copy-done.2 = s32[2,131072]{1,0:T(2,128)S(1)} copy-done((s32[2,131072]{1,0:T(2,128)S(1)}, s32[2,131072]{1,0:T(2,128)}, u32[]{:S(2)}) %copy-start.2) | copy-done | bytes 1048600
  17.0 0.0 copy-start.3
  17.0 1.0 %copy-done.3 = f32[131072]{0:T(1024)S(1)} copy-done((f32[131072]{0:T(1024)S(1)}, f32[131072]{0:T(1024)}, u32[]{:S(2)}) %copy-start.3) | copy-done | bytes 524312
  18.1 0.0 copy-start.1
  18.1 0.0 copy-start.4
  18.1 4.6 %pair_tables.1 = f32[96,128]{1,0:T(8,128)S(1)} custom-call(s32[2]{0:T(128)S(1)} %pad_add_fusion.rank_ref, s32[2,131072]{1,0:T(2,128)S(1)} %copy-done.2, f32[1,131072]{1,0:T(1,128)S(1)} %bitcast.8), custom_call_target="tpu_custom_call" | custom-call | flops 8589934592 | bytes 1572864 | tf_op jit(solution)/shard_map/pair_tables/pallas_call | solution.py:115
  22.7 0.0 collective-permute-done.5
  22.8 0.0 collective-permute-done.4
  22.8 0.0 collective-permute-done.3
  22.8 2.5 %collective-permute-start.6 = (f32[232,128]{1,0:T(8,128)S(1)}, f32[232,128]{1,0:T(8,128)S(1)}, u32[]{:S(2)}, u32[]{:S(2)}) collective-permute-start(f32[232,128]{1,0:T(8,128)S(1)} %pad_maximum_fusion), channel_id=1, source_target_pairs={{1,0},{2,1},{3,2},{0,3},{5,4},{6,5},{7,6},{4,7},{9,8},{10,9},{11,1... | collective-permute-start | bytes 356360 | tf_op jit(solution)/shard_map/ppermute | solution.py:549
  25.4 0.0 collective-permute-start.8
  25.4 1.7 %collective-permute-start.7 = (f32[232,128]{1,0:T(8,128)S(1)}, f32[232,128]{1,0:T(8,128)S(1)}, u32[]{:S(2)}, u32[]{:S(2)}) collective-permute-start(f32[232,128]{1,0:T(8,128)S(1)} %pad_maximum_fusion), channel_id=1, source_target_pairs={{2,0},{3,1},{0,2},{1,3},{6,4},{7,5},{4,6},{5,7},{10,8},{11,9},{8,1... | collective-permute-start | bytes 356360 | tf_op jit(solution)/shard_map/ppermute | solution.py:549
  27.1 0.1 collective-permute-done.6
  27.2 3.5 %collective-permute-done.7 = f32[232,128]{1,0:T(8,128)S(1)} collective-permute-done((f32[232,128]{1,0:T(8,128)S(1)}, f32[232,128]{1,0:T(8,128)S(1)}, u32[]{:S(2)}, u32[]{:S(2)}) %collective-permute-start.7) | collective-permute-done | bytes 118816 | tf_op jit(solution)/shard_map/ppermute | solution.py:549
  30.7 0.8 collective-permute-done.8
  31.6 6.0 %collective-permute-start.9 = (f32[776,128]{1,0:T(8,128)S(1)}, f32[776,128]{1,0:T(8,128)S(1)}, u32[]{:S(2)}, u32[]{:S(2)}) collective-permute-start(f32[776,128]{1,0:T(8,128)S(1)} %select_dynamic-update-slice_fusion.mine_ref), channel_id=1, source_target_pairs={{0,4},{4,0},{8,12},{12,8},{16,20},{20,16},{24,28},{28,24},{32,36},... | collective-permute-start | bytes 1191944 | tf_op jit(solution)/shard_map/ppermute | solution.py:526
  37.6 1.4 %collective-permute-done.9.other_ref = f32[776,128]{1,0:T(8,128)S(1)} collective-permute-done((f32[776,128]{1,0:T(8,128)S(1)}, f32[776,128]{1,0:T(8,128)S(1)}, u32[]{:S(2)}, u32[]{:S(2)}) %collective-permute-start.9) | collective-permute-done | bytes 397344 | tf_op jit(solution)/shard_map/ppermute | solution.py:526
  39.0 0.0 copy-done.1
  39.0 0.0 copy-done.4
  39.0 52.5 %panel_chain.1 = (f32[2,4096,128]{2,1,0:T(8,128)}, f32[4096,128]{1,0:T(8,128)}) custom-call(s32[2]{0:T(128)S(1)} %pad_add_fusion.rank_ref, f32[776,128]{1,0:T(8,128)S(1)} %select_dynamic-update-slice_fusion.mine_ref, f32[776,128]{1,0:T(8,128)S(1)} %collective-permute-done.9.other_ref, f32[1,128]{1,0:T(1,128)S(1)} %bitcast.9, f32[4096,128]{1,0:T(8,128)S(1)} %copy-done.1), custom_call_target="tpu_custom_call" | custom-call | flops 28991029248 | bytes 12582912 | tf_op jit(solution)/shard_map/panel_chain/pallas_call | solution.py:470
  (11 shorter events, 0.1 us)
Async XLA Ops:
  0.6 0.7 copy-start
  2.2 8.4 %collective-permute-start.2 = (f32[136,128]{1,0:T(8,128)S(1)}, f32[136,128]{1,0:T(8,128)S(1)}, u32[]{:S(2)}, u32[]{:S(2)}) collective-permute-start(f32[136,128]{1,0:T(8,128)S(1)} %pad_maximum_fusion.1), channel_id=1, source_target_pairs={{0,32},{4,36},{8,40},{1,33},{5,37},{9,41},{2,34},{6,38},{10,42},{3... | collective-permute-start | bytes 208904 | tf_op jit(solution)/shard_map/ppermute | solution.py:526
  6.6 4.0 %collective-permute-start.1 = (f32[136,128]{1,0:T(8,128)S(1)}, f32[136,128]{1,0:T(8,128)S(1)}, u32[]{:S(2)}, u32[]{:S(2)}) collective-permute-start(f32[136,128]{1,0:T(8,128)S(1)} %pad_maximum_fusion.1), channel_id=1, source_target_pairs={{0,64},{4,68},{8,72},{1,65},{5,69},{9,73},{2,66},{6,70},{10,74},{3... | collective-permute-start | bytes 208904 | tf_op jit(solution)/shard_map/ppermute | solution.py:526
  9.2 2.7 %collective-permute-start = (f32[136,128]{1,0:T(8,128)S(1)}, f32[136,128]{1,0:T(8,128)S(1)}, u32[]{:S(2)}, u32[]{:S(2)}) collective-permute-start(f32[136,128]{1,0:T(8,128)S(1)} %pad_maximum_fusion.1), channel_id=1, source_target_pairs={{0,96},{4,100},{8,104},{1,97},{5,101},{9,105},{2,98},{6,102},{10,1... | collective-permute-start | bytes 208904 | tf_op jit(solution)/shard_map/ppermute | solution.py:526
  11.9 10.8 %collective-permute-start.5 = (f32[136,128]{1,0:T(8,128)S(1)}, f32[136,128]{1,0:T(8,128)S(1)}, u32[]{:S(2)}, u32[]{:S(2)}) collective-permute-start(f32[136,128]{1,0:T(8,128)S(1)} %select_select_fusion.1), channel_id=1, source_target_pairs={{0,8},{4,12},{8,16},{32,40},{36,44},{40,48},{64,72},{68,76},{72,80... | collective-permute-start | bytes 208904 | tf_op jit(solution)/shard_map/ppermute | solution.py:526
  13.2 9.6 %collective-permute-start.4 = (f32[136,128]{1,0:T(8,128)S(1)}, f32[136,128]{1,0:T(8,128)S(1)}, u32[]{:S(2)}, u32[]{:S(2)}) collective-permute-start(f32[136,128]{1,0:T(8,128)S(1)} %select_select_fusion.1), channel_id=1, source_target_pairs={{0,16},{4,20},{8,24},{32,48},{36,52},{40,56},{64,80},{68,84},{72,8... | collective-permute-start | bytes 208904 | tf_op jit(solution)/shard_map/ppermute | solution.py:526
  14.5 8.3 %collective-permute-start.3 = (f32[136,128]{1,0:T(8,128)S(1)}, f32[136,128]{1,0:T(8,128)S(1)}, u32[]{:S(2)}, u32[]{:S(2)}) collective-permute-start(f32[136,128]{1,0:T(8,128)S(1)} %select_select_fusion.1), channel_id=1, source_target_pairs={{0,24},{4,28},{8,0},{32,56},{36,60},{40,32},{64,88},{68,92},{72,64... | collective-permute-start | bytes 208904 | tf_op jit(solution)/shard_map/ppermute | solution.py:526
  15.8 1.2 %copy-start.2 = (s32[2,131072]{1,0:T(2,128)S(1)}, s32[2,131072]{1,0:T(2,128)}, u32[]{:S(2)}) copy-start(s32[2,131072]{1,0:T(2,128)} %pairs_ref.1) | copy-start | bytes 3145732
  17.0 1.0 %copy-start.3 = (f32[131072]{0:T(1024)S(1)}, f32[131072]{0:T(1024)}, u32[]{:S(2)}) copy-start(f32[131072]{0:T(1024)} %param.9) | copy-start | bytes 1572868
  18.1 20.9 %copy-start.1 = (f32[4096,128]{1,0:T(8,128)S(1)}, f32[4096,128]{1,0:T(8,128)}, u32[]{:S(2)}) copy-start(f32[4096,128]{1,0:T(8,128)} %feat_hbm.1) | copy-start | bytes 6291460
  18.1 20.9 %copy-start.4 = (f32[128]{0:T(128)S(1)}, f32[128]{0:T(128)}, u32[]{:S(2)}) copy-start(f32[128]{0:T(128)} %param.6) | copy-start | bytes 1540
  22.8 4.4 %collective-permute-start.6 = (f32[232,128]{1,0:T(8,128)S(1)}, f32[232,128]{1,0:T(8,128)S(1)}, u32[]{:S(2)}, u32[]{:S(2)}) collective-permute-start(f32[232,128]{1,0:T(8,128)S(1)} %pad_maximum_fusion), channel_id=1, source_target_pairs={{1,0},{2,1},{3,2},{0,3},{5,4},{6,5},{7,6},{4,7},{9,8},{10,9},{11,1... | collective-permute-start | bytes 356360 | tf_op jit(solution)/shard_map/ppermute | solution.py:549
  25.4 6.2 %collective-permute-start.8 = (f32[232,128]{1,0:T(8,128)S(1)}, f32[232,128]{1,0:T(8,128)S(1)}, u32[]{:S(2)}, u32[]{:S(2)}) collective-permute-start(f32[232,128]{1,0:T(8,128)S(1)} %pad_maximum_fusion), channel_id=1, source_target_pairs={{3,0},{0,1},{1,2},{2,3},{7,4},{4,5},{5,6},{6,7},{11,8},{8,9},{9,10... | collective-permute-start | bytes 356360 | tf_op jit(solution)/shard_map/ppermute | solution.py:549
  25.4 5.3 %collective-permute-start.7 = (f32[232,128]{1,0:T(8,128)S(1)}, f32[232,128]{1,0:T(8,128)S(1)}, u32[]{:S(2)}, u32[]{:S(2)}) collective-permute-start(f32[232,128]{1,0:T(8,128)S(1)} %pad_maximum_fusion), channel_id=1, source_target_pairs={{2,0},{3,1},{0,2},{1,3},{6,4},{7,5},{4,6},{5,7},{10,8},{11,9},{8,1... | collective-permute-start | bytes 356360 | tf_op jit(solution)/shard_map/ppermute | solution.py:549
  31.6 7.4 %collective-permute-start.9 = (f32[776,128]{1,0:T(8,128)S(1)}, f32[776,128]{1,0:T(8,128)S(1)}, u32[]{:S(2)}, u32[]{:S(2)}) collective-permute-start(f32[776,128]{1,0:T(8,128)S(1)} %select_dynamic-update-slice_fusion.mine_ref), channel_id=1, source_target_pairs={{0,4},{4,0},{8,12},{12,8},{16,20},{20,16},{24,28},{28,24},{32,36},... | collective-permute-start | bytes 1191944 | tf_op jit(solution)/shard_map/ppermute | solution.py:526

commit v5 on v4

--- a/solution.py
+++ b/solution.py
@@ -51,7 +51,7 @@
     return high, (value - high.astype(f32)).astype(bf16)
 
 
-TABLE_CHUNK = 4096
+TABLE_CHUNK = 8192
 TABLE_ROWS = 96
 TABLE_SHARE = CONFIGS // 8
 QUARTER = BLOCK + 8
@@ -74,16 +74,15 @@
         one_hot = jnp.where(low_id == (place & 127), f32(1.0), f32(0.0)).astype(bf16)
         hit = code == (place >> 7)
         parts = [(offset >> 5).astype(f32), (offset & 31).astype(f32)]
-        parts += [part.astype(f32) for part in split3(weight)]
+        parts += [part.astype(f32) for part in split2(weight)]
         values = [jnp.where(hit, part, f32(0.0)) for part in parts]
-        values.append(jnp.zeros((8, TABLE_CHUNK), f32))
         acc_ref[...] += dot_nt(jnp.concatenate(values, 0).astype(bf16), one_hot)
         return carry
 
     lax.fori_loop(0, TABLE_SHARE // TABLE_CHUNK, step, 0)
     turned = acc_ref[...]
     offr = turned[0:40] * 32.0 + turned[40:80]
-    cr = turned[80:120] + turned[120:160] + turned[160:200]
+    cr = turned[80:120] + turned[120:160]
     out_ref[0:40, :] = offr
     out_ref[40:80, :] = cr
     offc = jnp.concatenate([offr.astype(i32), jnp.zeros((88, BLOCK), i32)], 0).T
@@ -120,7 +119,7 @@
             grid=(1,),
             in_specs=[pl.BlockSpec((2, TABLE_SHARE), share), pl.BlockSpec((1, TABLE_SHARE), share)],
             out_specs=pl.BlockSpec((TABLE_ROWS, BLOCK), lambda n, rank_ref: (0, 0)),
-            scratch_shapes=[pltpu.VMEM((208, BLOCK), f32)],
+            scratch_shapes=[pltpu.VMEM((160, BLOCK), f32)],
         ),
         out_shape=jax.ShapeDtypeStruct((TABLE_ROWS, BLOCK), f32),
         compiler_params=pltpu.CompilerParams(vmem_limit_bytes=VMEM_BYTES),

time: 92 us -> 91.2 us (level)
  transfers between devices with their start and end apart: 10 -> 10, of which waited for: 5 -> 5; matrix products, arithmetic and copies ran while one was open for 0% -> 0% of each run, Pallas kernels for 5% -> 4%
where the time goes in v5:
time: 91.2 us; the launch traced here: 90.8 us
  Pallas kernels  56.3 us (62%)
  starting transfers between devices  22.5 us (25%)
  waiting for transfers between devices  7.04 us (8%)
  local copies, waits for them, and re-layouts  3.85 us (4%)
  between operations  0.97 us (1%)
    pallas_call x1, Pallas kernels, panel_chain(): pl.pallas_call(chain_kernel, name='panel_chain', in_specs=[pl.BlockSpec(m...  52.5 us
    ppermute x7, starting transfers between devices, send(): return lax.ppermute(value, 'row', pairs)  18.2 us
    ppermute x3, waiting for transfers between devices, share_panels(): lax.ppermute(part, 'col', [((i + k) % 4, i) for i in range(4)])  4.43 us
    ppermute x3, starting transfers between devices, share_panels(): lax.ppermute(part, 'col', [((i + k) % 4, i) for i in range(4)])  4.27 us
    pallas_call x1, Pallas kernels, pair_tables(): pl.pallas_call(tables_kernel, name='pair_tables', grid_spec=pltpu.Prefetc...  3.8 us
    unnamed x13, local copies, waits for them, and re-layouts  3 us
    ppermute x7, waiting for transfers between devices, send(): return lax.ppermute(value, 'row', pairs)  2.61 us
  transfers between devices with their start and end apart: 10, of which 5 were waited for; matrix products, arithmetic and copies ran while one was open for 0% of the time, Pallas kernels for 4%

profile of v5, /device:TPU:1, one launch (start us, length us, event | category | flops | bytes accessed | tf_op | source)
XLA Modules:
  0.0 90.8 jit_solution(8422279346142770710)
XLA Ops:
  0.6 0.0 copy-start
  0.6 0.7 copy-done
  1.4 0.8 constant_dynamic-slice_fusion
  2.2 4.4 %collective-permute-start.2 = (f32[136,128]{1,0:T(8,128)S(1)}, f32[136,128]{1,0:T(8,128)S(1)}, u32[]{:S(2)}, u32[]{:S(2)}) collective-permute-start(f32[136,128]{1,0:T(8,128)S(1)} %pad_maximum_fusion.1), channel_id=1, source_target_pairs={{0,32},{4,36},{8,40},{1,33},{5,37},{9,41},{2,34},{6,38},{10,42},{3... | collective-permute-start | bytes 208904 | tf_op jit(solution)/shard_map/ppermute | solution.py:525
  6.6 2.6 %collective-permute-start.1 = (f32[136,128]{1,0:T(8,128)S(1)}, f32[136,128]{1,0:T(8,128)S(1)}, u32[]{:S(2)}, u32[]{:S(2)}) collective-permute-start(f32[136,128]{1,0:T(8,128)S(1)} %pad_maximum_fusion.1), channel_id=1, source_target_pairs={{0,64},{4,68},{8,72},{1,65},{5,69},{9,73},{2,66},{6,70},{10,74},{3... | collective-permute-start | bytes 208904 | tf_op jit(solution)/shard_map/ppermute | solution.py:525
  9.2 1.3 %collective-permute-start = (f32[136,128]{1,0:T(8,128)S(1)}, f32[136,128]{1,0:T(8,128)S(1)}, u32[]{:S(2)}, u32[]{:S(2)}) collective-permute-start(f32[136,128]{1,0:T(8,128)S(1)} %pad_maximum_fusion.1), channel_id=1, source_target_pairs={{0,96},{4,100},{8,104},{1,97},{5,101},{9,105},{2,98},{6,102},{10,1... | collective-permute-start | bytes 208904 | tf_op jit(solution)/shard_map/ppermute | solution.py:525
  10.6 0.1 pad_add_fusion.rank_ref
  10.6 0.0 collective-permute-done.2
  10.6 0.0 collective-permute-done.1
  10.6 1.2 %collective-permute-done = f32[136,128]{1,0:T(8,128)S(1)} collective-permute-done((f32[136,128]{1,0:T(8,128)S(1)}, f32[136,128]{1,0:T(8,128)S(1)}, u32[]{:S(2)}, u32[]{:S(2)}) %collective-permute-start) | collective-permute-done | bytes 69664 | tf_op jit(solution)/shard_map/ppermute | solution.py:525
  11.9 1.3 %collective-permute-start.5 = (f32[136,128]{1,0:T(8,128)S(1)}, f32[136,128]{1,0:T(8,128)S(1)}, u32[]{:S(2)}, u32[]{:S(2)}) collective-permute-start(f32[136,128]{1,0:T(8,128)S(1)} %select_select_fusion.1), channel_id=1, source_target_pairs={{0,8},{4,12},{8,16},{32,40},{36,44},{40,48},{64,72},{68,76},{72,80... | collective-permute-start | bytes 208904 | tf_op jit(solution)/shard_map/ppermute | solution.py:525
  13.2 1.3 %collective-permute-start.4 = (f32[136,128]{1,0:T(8,128)S(1)}, f32[136,128]{1,0:T(8,128)S(1)}, u32[]{:S(2)}, u32[]{:S(2)}) collective-permute-start(f32[136,128]{1,0:T(8,128)S(1)} %select_select_fusion.1), channel_id=1, source_target_pairs={{0,16},{4,20},{8,24},{32,48},{36,52},{40,56},{64,80},{68,84},{72,8... | collective-permute-start | bytes 208904 | tf_op jit(solution)/shard_map/ppermute | solution.py:525
  14.5 1.3 %collective-permute-start.3 = (f32[136,128]{1,0:T(8,128)S(1)}, f32[136,128]{1,0:T(8,128)S(1)}, u32[]{:S(2)}, u32[]{:S(2)}) collective-permute-start(f32[136,128]{1,0:T(8,128)S(1)} %select_select_fusion.1), channel_id=1, source_target_pairs={{0,24},{4,28},{8,0},{32,56},{36,60},{40,32},{64,88},{68,92},{72,64... | collective-permute-start | bytes 208904 | tf_op jit(solution)/shard_map/ppermute | solution.py:525
  15.8 0.0 copy-start.2
  15.8 1.2 %copy-done.2 = s32[2,131072]{1,0:T(2,128)S(1)} copy-done((s32[2,131072]{1,0:T(2,128)S(1)}, s32[2,131072]{1,0:T(2,128)}, u32[]{:S(2)}) %copy-start.2) | copy-done | bytes 1048600
  17.0 0.0 copy-start.3
  17.0 1.0 %copy-done.3 = f32[131072]{0:T(1024)S(1)} copy-done((f32[131072]{0:T(1024)S(1)}, f32[131072]{0:T(1024)}, u32[]{:S(2)}) %copy-start.3) | copy-done | bytes 524312
  18.1 0.0 copy-start.1
  18.1 0.0 copy-start.4
  18.1 3.8 %pair_tables.1 = f32[96,128]{1,0:T(8,128)S(1)} custom-call(s32[2]{0:T(128)S(1)} %pad_add_fusion.rank_ref, s32[2,131072]{1,0:T(2,128)S(1)} %copy-done.2, f32[1,131072]{1,0:T(1,128)S(1)} %bitcast.8), custom_call_target="tpu_custom_call" | custom-call | flops 8589934592 | bytes 1572864 | tf_op jit(solution)/shard_map/pair_tables/pallas_call | solution.py:114
  21.9 0.0 collective-permute-done.5
  21.9 0.0 collective-permute-done.4
  21.9 0.0 collective-permute-done.3
  22.0 2.5 %collective-permute-start.6 = (f32[232,128]{1,0:T(8,128)S(1)}, f32[232,128]{1,0:T(8,128)S(1)}, u32[]{:S(2)}, u32[]{:S(2)}) collective-permute-start(f32[232,128]{1,0:T(8,128)S(1)} %pad_maximum_fusion), channel_id=1, source_target_pairs={{1,0},{2,1},{3,2},{0,3},{5,4},{6,5},{7,6},{4,7},{9,8},{10,9},{11,1... | collective-permute-start | bytes 356360 | tf_op jit(solution)/shard_map/ppermute | solution.py:548
  24.5 0.0 collective-permute-start.8
  24.5 1.7 %collective-permute-start.7 = (f32[232,128]{1,0:T(8,128)S(1)}, f32[232,128]{1,0:T(8,128)S(1)}, u32[]{:S(2)}, u32[]{:S(2)}) collective-permute-start(f32[232,128]{1,0:T(8,128)S(1)} %pad_maximum_fusion), channel_id=1, source_target_pairs={{2,0},{3,1},{0,2},{1,3},{6,4},{7,5},{4,6},{5,7},{10,8},{11,9},{8,1... | collective-permute-start | bytes 356360 | tf_op jit(solution)/shard_map/ppermute | solution.py:548
  26.3 0.1 collective-permute-done.6
  26.4 3.5 %collective-permute-done.7 = f32[232,128]{1,0:T(8,128)S(1)} collective-permute-done((f32[232,128]{1,0:T(8,128)S(1)}, f32[232,128]{1,0:T(8,128)S(1)}, u32[]{:S(2)}, u32[]{:S(2)}) %collective-permute-start.7) | collective-permute-done | bytes 118816 | tf_op jit(solution)/shard_map/ppermute | solution.py:548
  29.9 0.8 collective-permute-done.8
  30.8 6.0 %collective-permute-start.9 = (f32[776,128]{1,0:T(8,128)S(1)}, f32[776,128]{1,0:T(8,128)S(1)}, u32[]{:S(2)}, u32[]{:S(2)}) collective-permute-start(f32[776,128]{1,0:T(8,128)S(1)} %select_dynamic-update-slice_fusion.mine_ref), channel_id=1, source_target_pairs={{0,4},{4,0},{8,12},{12,8},{16,20},{20,16},{24,28},{28,24},{32,36},... | collective-permute-start | bytes 1191944 | tf_op jit(solution)/shard_map/ppermute | solution.py:525
  36.8 1.4 %collective-permute-done.9.other_ref = f32[776,128]{1,0:T(8,128)S(1)} collective-permute-done((f32[776,128]{1,0:T(8,128)S(1)}, f32[776,128]{1,0:T(8,128)S(1)}, u32[]{:S(2)}, u32[]{:S(2)}) %collective-permute-start.9) | collective-permute-done | bytes 397344 | tf_op jit(solution)/shard_map/ppermute | solution.py:525
  38.2 0.0 copy-done.1
  38.2 0.0 copy-done.4
  38.2 52.5 %panel_chain.1 = (f32[2,4096,128]{2,1,0:T(8,128)}, f32[4096,128]{1,0:T(8,128)}) custom-call(s32[2]{0:T(128)S(1)} %pad_add_fusion.rank_ref, f32[776,128]{1,0:T(8,128)S(1)} %select_dynamic-update-slice_fusion.mine_ref, f32[776,128]{1,0:T(8,128)S(1)} %collective-permute-done.9.other_ref, f32[1,128]{1,0:T(1,128)S(1)} %bitcast.9, f32[4096,128]{1,0:T(8,128)S(1)} %copy-done.1), custom_call_target="tpu_custom_call" | custom-call | flops 28991029248 | bytes 12582912 | tf_op jit(solution)/shard_map/panel_chain/pallas_call | solution.py:469
  (11 shorter events, 0.1 us)
Async XLA Ops:
  0.6 0.7 copy-start
  2.2 8.4 %collective-permute-start.2 = (f32[136,128]{1,0:T(8,128)S(1)}, f32[136,128]{1,0:T(8,128)S(1)}, u32[]{:S(2)}, u32[]{:S(2)}) collective-permute-start(f32[136,128]{1,0:T(8,128)S(1)} %pad_maximum_fusion.1), channel_id=1, source_target_pairs={{0,32},{4,36},{8,40},{1,33},{5,37},{9,41},{2,34},{6,38},{10,42},{3... | collective-permute-start | bytes 208904 | tf_op jit(solution)/shard_map/ppermute | solution.py:525
  6.6 4.0 %collective-permute-start.1 = (f32[136,128]{1,0:T(8,128)S(1)}, f32[136,128]{1,0:T(8,128)S(1)}, u32[]{:S(2)}, u32[]{:S(2)}) collective-permute-start(f32[136,128]{1,0:T(8,128)S(1)} %pad_maximum_fusion.1), channel_id=1, source_target_pairs={{0,64},{4,68},{8,72},{1,65},{5,69},{9,73},{2,66},{6,70},{10,74},{3... | collective-permute-start | bytes 208904 | tf_op jit(solution)/shard_map/ppermute | solution.py:525
  9.2 2.7 %collective-permute-start = (f32[136,128]{1,0:T(8,128)S(1)}, f32[136,128]{1,0:T(8,128)S(1)}, u32[]{:S(2)}, u32[]{:S(2)}) collective-permute-start(f32[136,128]{1,0:T(8,128)S(1)} %pad_maximum_fusion.1), channel_id=1, source_target_pairs={{0,96},{4,100},{8,104},{1,97},{5,101},{9,105},{2,98},{6,102},{10,1... | collective-permute-start | bytes 208904 | tf_op jit(solution)/shard_map/ppermute | solution.py:525
  11.9 10.0 %collective-permute-start.5 = (f32[136,128]{1,0:T(8,128)S(1)}, f32[136,128]{1,0:T(8,128)S(1)}, u32[]{:S(2)}, u32[]{:S(2)}) collective-permute-start(f32[136,128]{1,0:T(8,128)S(1)} %select_select_fusion.1), channel_id=1, source_target_pairs={{0,8},{4,12},{8,16},{32,40},{36,44},{40,48},{64,72},{68,76},{72,80... | collective-permute-start | bytes 208904 | tf_op jit(solution)/shard_map/ppermute | solution.py:525
  13.2 8.7 %collective-permute-start.4 = (f32[136,128]{1,0:T(8,128)S(1)}, f32[136,128]{1,0:T(8,128)S(1)}, u32[]{:S(2)}, u32[]{:S(2)}) collective-permute-start(f32[136,128]{1,0:T(8,128)S(1)} %select_select_fusion.1), channel_id=1, source_target_pairs={{0,16},{4,20},{8,24},{32,48},{36,52},{40,56},{64,80},{68,84},{72,8... | collective-permute-start | bytes 208904 | tf_op jit(solution)/shard_map/ppermute | solution.py:525
  14.5 7.4 %collective-permute-start.3 = (f32[136,128]{1,0:T(8,128)S(1)}, f32[136,128]{1,0:T(8,128)S(1)}, u32[]{:S(2)}, u32[]{:S(2)}) collective-permute-start(f32[136,128]{1,0:T(8,128)S(1)} %select_select_fusion.1), channel_id=1, source_target_pairs={{0,24},{4,28},{8,0},{32,56},{36,60},{40,32},{64,88},{68,92},{72,64... | collective-permute-start | bytes 208904 | tf_op jit(solution)/shard_map/ppermute | solution.py:525
  15.8 1.2 %copy-start.2 = (s32[2,131072]{1,0:T(2,128)S(1)}, s32[2,131072]{1,0:T(2,128)}, u32[]{:S(2)}) copy-start(s32[2,131072]{1,0:T(2,128)} %pairs_ref.1) | copy-start | bytes 3145732
  17.0 1.0 %copy-start.3 = (f32[131072]{0:T(1024)S(1)}, f32[131072]{0:T(1024)}, u32[]{:S(2)}) copy-start(f32[131072]{0:T(1024)} %param.9) | copy-start | bytes 1572868
  18.1 20.1 %copy-start.1 = (f32[4096,128]{1,0:T(8,128)S(1)}, f32[4096,128]{1,0:T(8,128)}, u32[]{:S(2)}) copy-start(f32[4096,128]{1,0:T(8,128)} %feat_hbm.1) | copy-start | bytes 6291460
  18.1 20.1 %copy-start.4 = (f32[128]{0:T(128)S(1)}, f32[128]{0:T(128)}, u32[]{:S(2)}) copy-start(f32[128]{0:T(128)} %param.6) | copy-start | bytes 1540
  22.0 4.4 %collective-permute-start.6 = (f32[232,128]{1,0:T(8,128)S(1)}, f32[232,128]{1,0:T(8,128)S(1)}, u32[]{:S(2)}, u32[]{:S(2)}) collective-permute-start(f32[232,128]{1,0:T(8,128)S(1)} %pad_maximum_fusion), channel_id=1, source_target_pairs={{1,0},{2,1},{3,2},{0,3},{5,4},{6,5},{7,6},{4,7},{9,8},{10,9},{11,1... | collective-permute-start | bytes 356360 | tf_op jit(solution)/shard_map/ppermute | solution.py:548
  24.5 6.2 %collective-permute-start.8 = (f32[232,128]{1,0:T(8,128)S(1)}, f32[232,128]{1,0:T(8,128)S(1)}, u32[]{:S(2)}, u32[]{:S(2)}) collective-permute-start(f32[232,128]{1,0:T(8,128)S(1)} %pad_maximum_fusion), channel_id=1, source_target_pairs={{3,0},{0,1},{1,2},{2,3},{7,4},{4,5},{5,6},{6,7},{11,8},{8,9},{9,10... | collective-permute-start | bytes 356360 | tf_op jit(solution)/shard_map/ppermute | solution.py:548
  24.5 5.3 %collective-permute-start.7 = (f32[232,128]{1,0:T(8,128)S(1)}, f32[232,128]{1,0:T(8,128)S(1)}, u32[]{:S(2)}, u32[]{:S(2)}) collective-permute-start(f32[232,128]{1,0:T(8,128)S(1)} %pad_maximum_fusion), channel_id=1, source_target_pairs={{2,0},{3,1},{0,2},{1,3},{6,4},{7,5},{4,6},{5,7},{10,8},{11,9},{8,1... | collective-permute-start | bytes 356360 | tf_op jit(solution)/shard_map/ppermute | solution.py:548
  30.8 7.4 %collective-permute-start.9 = (f32[776,128]{1,0:T(8,128)S(1)}, f32[776,128]{1,0:T(8,128)S(1)}, u32[]{:S(2)}, u32[]{:S(2)}) collective-permute-start(f32[776,128]{1,0:T(8,128)S(1)} %select_dynamic-update-slice_fusion.mine_ref), channel_id=1, source_target_pairs={{0,4},{4,0},{8,12},{12,8},{16,20},{20,16},{24,28},{28,24},{32,36},... | collective-permute-start | bytes 1191944 | tf_op jit(solution)/shard_map/ppermute | solution.py:525
